TPU v7x, 512 devices: a whole 4x8x8 slice. The times are simulated.
512 devices in a mesh: space: 16 (over z, core), dp: 32 (over y, x).
Axes of the slice: x: 4, y: 8, z: 8, core: 2. Of those that a mesh axis runs over, the one named last changes fastest.
Arguments:
- volumes: bfloat16 [32, 64, 32, 16, 128], P('dp', None, 'space'), may hold values from -6 to 6
- w_first: bfloat16 [3, 3, 3, 64, 64], replicated, may hold values from -0.15625 to 0.15625
- w_down: bfloat16 [2, 2, 2, 64, 64], replicated, may hold values from -0.25 to 0.25
- w_coarse: bfloat16 [3, 3, 3, 64, 64], replicated, may hold values from -0.15625 to 0.15625
- coarse_cotangent: bfloat16 [32, 64, 16, 8, 64], P('dp', None, 'space'), may hold values from -6 to 6
Outputs:
- coarse_out: bfloat16 [32, 64, 16, 8, 64], P('dp', None, 'space')
- grad_first: float32 [3, 3, 3, 64, 64], replicated
- grad_down: float32 [2, 2, 2, 64, 64], replicated
- grad_coarse: float32 [3, 3, 3, 64, 64], replicated
All inputs are finite; a program needn't handle non-finite values.
Results may differ from a plain program's by a relative error of at most 0.015.
Values may be sent and summed in bfloat16 or wider, within the bound.
No kernel may reach another device: no remote copies, remote signals or barrier semaphores. Data moves between devices by JAX's collectives and lax.ppermute only.
A program may use at most 64 MiB of HBM per device.

v0:
```python
import jax
import jax.numpy as jnp
from jax import lax
from jax.sharding import PartitionSpec as P

conv_layout = ("NCDHW", "DHWIO", "NCDHW")


def padded_2(cells, sides, width):
    for axis, dim in sides:
        count = lax.axis_size(axis)
        ends = count - 1
        head = lax.slice_in_dim(cells, 0, width, axis=dim)
        tail = lax.slice_in_dim(cells, cells.shape[dim] - width, cells.shape[dim], axis=dim)
        cells = jnp.concatenate(
            [
                lax.ppermute(tail, axis, [(i, (i + 1) % count) for i in range(ends)]),
                cells,
                lax.ppermute(head, axis, [((i + 1) % count, i) for i in range(ends)]),
            ],
            axis=dim,
        )
    return cells


def pad_plane(field):
    return jnp.pad(field, ((0, 0), (0, 0), (0, 0), (1, 1), (1, 1)))


def conv_cube(padded, weight):
    return lax.conv_general_dilated(
        padded,
        weight,
        (1, 1, 1),
        "VALID",
        dimension_numbers=conv_layout,
        preferred_element_type=jnp.float32,
    )


def conv_down(field, weight):
    return lax.conv_general_dilated(
        field,
        weight,
        (2, 2, 2),
        "VALID",
        dimension_numbers=conv_layout,
        preferred_element_type=jnp.float32,
    )


def kernel_grad(padded, grads, dilation):
    return lax.conv_general_dilated(
        padded,
        grads,
        (1, 1, 1),
        "VALID",
        rhs_dilation=dilation,
        dimension_numbers=("CNDHW", "IODHW", "DHWNC"),
        preferred_element_type=jnp.float32,
    )


def silu_slope(value):
    sigmoid_val = jax.nn.sigmoid(value)
    return sigmoid_val * (1.0 + value * (1.0 - sigmoid_val))


def flipped(weight):
    return jnp.swapaxes(weight[::-1, ::-1, ::-1], 3, 4)


def up_sample(grads, weight):
    spread = jnp.einsum("bopqr,xyzio->bipxqyrz", grads, weight, preferred_element_type=jnp.float32)
    shape = grads.shape
    return spread.reshape(shape[0], weight.shape[3], 2 * shape[2], 2 * shape[3], 2 * shape[4])


def coarse_pad(field):
    return pad_plane(padded_2(field, (("space", 2),), 1))


def local(volumes, w_first, w_down, w_coarse, coarse_cotangent):
    padded_in = pad_plane(padded_2(volumes, (("space", 2),), 1))
    first_pre = conv_cube(padded_in, w_first)
    first_act = jax.nn.silu(first_pre).astype(jnp.bfloat16)
    down_out = conv_down(first_act, w_down).astype(jnp.bfloat16)
    padded_down = coarse_pad(down_out)
    coarse_pre = conv_cube(padded_down, w_coarse)
    coarse_out = jax.nn.silu(coarse_pre).astype(jnp.bfloat16)
    coarse_grad = (coarse_cotangent.astype(jnp.float32) * silu_slope(coarse_pre)).astype(
        jnp.bfloat16
    )
    down_grad = conv_cube(coarse_pad(coarse_grad), flipped(w_coarse)).astype(jnp.bfloat16)
    grad_coarse = kernel_grad(padded_down, coarse_grad, (1, 1, 1))
    grad_down = kernel_grad(first_act, down_grad, (2, 2, 2))
    first_grad = (up_sample(down_grad, w_down) * silu_slope(first_pre)).astype(jnp.bfloat16)
    grad_first = kernel_grad(padded_in, first_grad, (1, 1, 1))
    grad_first, grad_down, grad_coarse = lax.psum(
        (grad_first, grad_down, grad_coarse), ("space", "dp")
    )
    return (coarse_out, grad_first, grad_down, grad_coarse)


def solution(mesh):
    return jax.shard_map(
        local,
        mesh=mesh,
        in_specs=(
            P("dp", None, "space", None, None),
            P(),
            P(),
            P(),
            P("dp", None, "space", None, None),
        ),
        out_specs=(P("dp", None, "space", None, None), P(), P(), P()),
        check_vma=False,
    )
```

profile of v0, /device:TPU:1, one launch (start us, length us, event | category | flops | bytes accessed | tf_op | source)
XLA Modules:
  0.0 411.6 jit_solution(1636104162368238329)
XLA Ops:
  7.2 1.1 fusion.73
  8.3 5.4 %collective-permute-start = (bf16[1,64,1,16,128]{4,3,2,1,0:T(8,128)(2,1)S(1)}, bf16[1,64,1,16,128]{4,3,2,1,0:T(8,128)(2,1)S(1)}, u32[]{:S(2)}, u32[]{:S(2)}) collective-permute-start(bf16[1,64,1,16,128]{4,3,2,1,0:T(8,128)(2,1)S(1)} %get-tuple-element.20), channel_id=1, source_target_pairs={{0,32},{32,64},{64,96},{96,128},{128,160},{160,192},{192,224},{224... | collective-permute-start | bytes 786440 | tf_op jit(solution)/shard_map/ppermute | solution.py:17
  13.7 4.7 %collective-permute-start.1 = (bf16[1,64,1,16,128]{4,3,2,1,0:T(8,128)(2,1)S(1)}, bf16[1,64,1,16,128]{4,3,2,1,0:T(8,128)(2,1)S(1)}, u32[]{:S(2)}, u32[]{:S(2)}) collective-permute-start(bf16[1,64,1,16,128]{4,3,2,1,0:T(8,128)(2,1)S(1)} %get-tuple-element.19), channel_id=1, source_target_pairs={{32,0},{64,32},{96,64},{128,96},{160,128},{192,160},{224,192},{256... | collective-permute-start | bytes 786440 | tf_op jit(solution)/shard_map/ppermute | solution.py:19
  18.4 1.1 copy.63
  19.6 1.1 constant_dynamic-update-slice_fusion.1
  20.7 0.7 collective-permute-done.1
  21.5 1.0 copy-done.1
  22.5 3.7 copy.83
  26.2 0.4 pad.5.clone
  26.6 0.6 copy.51
  27.3 4.5 %broadcast_select_fusion = (bf16[2,16,8,17,64]{4,2,3,1,0:T(8,128)(2,1)S(1)}, bf16[2,16,8,17,64]{4,2,3,1,0:T(8,128)(2,1)S(1)}, f32[2,16,8,17,64]{4,2,3,1,0:T(8,128)S(1)}) fusion(pred[8,17]{0,1:T(8,128)(4,1)S(1)} %copy-done.11, bf16[3,3,3,64,64]{4,3,2,1,0:T(8,128)(2,1)S(1)} %copy-done, bf16[64,4,16,1,7,2]{0,4,5,2,1,3:T(8,128)(2,1)S(1)} %slice.20, ...), kind=kOutput, calls=%fused_computation.39 | convolution fusion | flops 928169984 | bytes 3678344 | tf_op jit(solution)/shard_map/conv_general_dilated | solution.py:31
  31.8 0.1 copy.52
  32.0 0.2 slice.21
  32.2 0.3 copy.53
  32.5 0.3 copy.55
  32.8 0.3 copy-done.9
  33.1 0.4 convolution_convert_fusion
  33.5 0.2 copy.103
  33.8 1.9 collective-permute-start.3
  35.7 3.8 collective-permute-start.2
  39.7 0.2 pad.12
  39.9 0.3 copy-done.12
  40.2 1.5 fusion.33
  41.8 0.8 add_multiply_fusion
  42.6 1.3 fusion.20
  43.9 7.5 %copy.72 = bf16[1,64,4,16,128]{1,0,4,3,2:T(2,128)(2,1)} copy(bf16[1,64,4,16,128]{4,3,2,1,0:T(8,128)(2,1)} %copy-done.1) | data formatting | bytes 2097152 | tf_op jit(solution)/shard_map/concatenate | solution.py:15
  51.4 0.4 copy.70
  52.0 0.7 copy-done.7
  52.8 2.7 pad_maximum_fusion
  55.5 1.7 copy.58
  57.2 2.1 copy.84
  59.3 1.1 pad.8.clone
  60.5 2.4 add_multiply_fusion.1
  63.0 1.9 collective-permute-start.5
  64.9 3.9 collective-permute-start.4
  68.8 4.9 %fusion.52 = f32[3,3,3,64,64]{4,3,2,1,0:T(8,128)} fusion(bf16[1,64,3,8,64]{1,0,4,3,2:T(2,128)(2,1)S(1)} %pad_maximum_fusion, bf16[1,64,1,8,64]{1,3,4,0,2:T(8,128)(2,1)S(1)} %fusion.51), kind=kOutput, calls=%fused_computation.67 | convolution fusion | flops 102727680 | bytes 704512 | tf_op jit(solution)/shard_map/conv_general_dilated | solution.py:53
  74.0 0.7 copy-done.13
  74.7 1.2 fusion.24
  75.9 0.5 convolution_bitcast_fusion
  76.4 1.7 copy.69
  78.1 1.2 fusion.21
  79.3 1.7 fusion.15
  81.1 32.7 %fusion.16 = f32[3,3,3,64,64]{4,3,2,1,0:T(8,128)} fusion(bf16[1,64,4,16,128]{1,0,4,3,2:T(2,128)(2,1)} %copy.72, bf16[1,64,2,16,128]{1,4,3,2,0:T(8,128)(2,1)} %fusion.15), kind=kOutput, calls=%fused_computation.22 | convolution fusion | flops 863698944 | bytes 2015232 | tf_op jit(solution)/shard_map/conv_general_dilated | solution.py:53
  113.9 0.8 copy.79
  114.7 285.0 %all-reduce.3.cloned.1.call-done = (f32[3,3,3,64,64]{4,3,2,1,0:T(8,128)}, f32[2,2,2,64,64]{4,3,2,1,0:T(8,128)}, f32[3,3,3,64,64]{4,3,2,1,0:T(8,128)}) async-done(((f32[3,3,3,64,64]{4,3,2,1,0:T(8,128)}, f32[2,2,2,64,64]{4,3,2,1,0:T(8,128)}, f32[3,3,3,64,64]{4,3,2,1,0:T(8,128)}), (f32[3,3,3,64,64]{4,3,2,1,0:T(8,128)}, f32[2,2,2,64,64]{4,3,2,1,0:T(8,128)}, ...) | async-done | bytes 1015824 | tf_op jit(solution)/shard_map/psum | solution.py:99
  399.7 2.3 copy.110
  402.0 1.7 copy.111
  403.6 0.9 copy.112
  (53 shorter events, 1.3 us)
Async XLA Ops:
  7.2 20.1 %copy-start = (bf16[3,3,3,64,64]{4,3,2,1,0:T(8,128)(2,1)S(1)}, bf16[3,3,3,64,64]{4,3,2,1,0:T(8,128)(2,1)}, u32[]{:S(2)}) copy-start(bf16[3,3,3,64,64]{4,3,2,1,0:T(8,128)(2,1)} %param.6) | copy-start | bytes 663556
  7.2 392.5 %all-reduce.3.cloned.1.call-start = ((), (), s32[]{:S(2)}) async-start(), calls=%async_computation | async-start | bytes 4063232 | tf_op jit(solution)/shard_map/psum | solution.py:99
  8.3 11.2 %collective-permute-start = (bf16[1,64,1,16,128]{4,3,2,1,0:T(8,128)(2,1)S(1)}, bf16[1,64,1,16,128]{4,3,2,1,0:T(8,128)(2,1)S(1)}, u32[]{:S(2)}, u32[]{:S(2)}) collective-permute-start(bf16[1,64,1,16,128]{4,3,2,1,0:T(8,128)(2,1)S(1)} %get-tuple-element.20), channel_id=1, source_target_pairs={{0,32},{32,64},{64,96},{96,128},{128,160},{160,192},{192,224},{224... | collective-permute-start | bytes 786440 | tf_op jit(solution)/shard_map/ppermute | solution.py:17
  13.7 7.7 %collective-permute-start.1 = (bf16[1,64,1,16,128]{4,3,2,1,0:T(8,128)(2,1)S(1)}, bf16[1,64,1,16,128]{4,3,2,1,0:T(8,128)(2,1)S(1)}, u32[]{:S(2)}, u32[]{:S(2)}) collective-permute-start(bf16[1,64,1,16,128]{4,3,2,1,0:T(8,128)(2,1)S(1)} %get-tuple-element.19), channel_id=1, source_target_pairs={{32,0},{64,32},{96,64},{128,96},{160,128},{192,160},{224,192},{256... | collective-permute-start | bytes 786440 | tf_op jit(solution)/shard_map/ppermute | solution.py:19
  21.5 1.0 copy-start.1
  26.6 0.7 copy-start.11
  32.2 0.9 copy-start.9
  33.8 6.2 %copy-start.4 = (bf16[1,8,1,64,64]{4,2,3,1,0:T(2,128)(2,1)}, bf16[1,8,1,64,64]{4,2,3,1,0:T(2,128)(2,1)S(1)}, u32[]{:S(2)}) copy-start(bf16[1,8,1,64,64]{4,2,3,1,0:T(2,128)(2,1)S(1)} %copy.103) | copy-start | bytes 196612
  33.8 18.2 %collective-permute-start.3 = (bf16[1,64,1,8,64]{1,0,4,3,2:T(2,128)(2,1)S(1)}, bf16[1,64,1,8,64]{1,0,4,3,2:T(2,128)(2,1)S(1)}, u32[]{:S(2)}, u32[]{:S(2)}) collective-permute-start(bf16[1,64,1,8,64]{1,0,4,3,2:T(2,128)(2,1)S(1)} %bitcast.103), channel_id=1, source_target_pairs={{32,0},{64,32},{96,64},{128,96},{160,128},{192,160},{224,192},{256... | collective-permute-start | bytes 196616 | tf_op jit(solution)/shard_map/ppermute | solution.py:19
  35.7 17.0 %collective-permute-start.2 = (bf16[1,64,1,8,64]{1,0,4,3,2:T(2,128)(2,1)S(1)}, bf16[1,64,1,8,64]{1,0,4,3,2:T(2,128)(2,1)}, u32[]{:S(2)}, u32[]{:S(2)}) collective-permute-start(bf16[1,64,1,8,64]{1,0,4,3,2:T(2,128)(2,1)S(1)} %bitcast.104), channel_id=1, source_target_pairs={{0,32},{32,64},{64,96},{96,128},{128,160},{160,192},{192,224},{224... | collective-permute-start | bytes 196616 | tf_op jit(solution)/shard_map/ppermute | solution.py:17
  39.5 0.7 copy-start.12
  51.9 1.0 copy-start.5
  52.0 0.7 copy-start.7
  55.5 4.9 %copy-start.14 = (pred[8,9]{0,1:T(8,128)(4,1)S(1)}, pred[8,9]{0,1:T(8,128)(4,1)}, u32[]{:S(2)}) copy-start(pred[8,9]{0,1:T(8,128)(4,1)} %constant.31) | copy-start | bytes 220
  63.0 10.7 %collective-permute-start.5 = (bf16[1,64,1,8,64]{1,3,4,0,2:T(8,128)(2,1)S(1)}, bf16[1,64,1,8,64]{1,3,4,0,2:T(8,128)(2,1)S(1)}, u32[]{:S(2)}, u32[]{:S(2)}) collective-permute-start(bf16[1,64,1,8,64]{1,3,4,0,2:T(8,128)(2,1)S(1)} %fusion.51), channel_id=1, source_target_pairs={{32,0},{64,32},{96,64},{128,96},{160,128},{192,160},{224,192},{256... | collective-permute-start | bytes 196616 | tf_op jit(solution)/shard_map/ppermute | solution.py:19
  64.9 8.7 %collective-permute-start.4 = (bf16[1,64,1,8,64]{1,3,4,0,2:T(8,128)(2,1)S(1)}, bf16[1,64,1,8,64]{1,3,4,0,2:T(8,128)(2,1)S(1)}, u32[]{:S(2)}, u32[]{:S(2)}) collective-permute-start(bf16[1,64,1,8,64]{1,3,4,0,2:T(8,128)(2,1)S(1)} %fusion.51), channel_id=1, source_target_pairs={{0,32},{32,64},{64,96},{96,128},{128,160},{160,192},{192,224},{224... | collective-permute-start | bytes 196616 | tf_op jit(solution)/shard_map/ppermute | solution.py:17
  73.6 1.0 copy-start.13
  73.9 2.0 copy-start.10
  76.4 1.7 copy-start.2
  76.4 1.7 copy-start.3
  81.1 32.8 %copy-start.8 = (bf16[1,8,8,9,64]{4,2,3,1,0:T(8,128)(2,1)S(1)}, bf16[1,8,8,9,64]{4,2,3,1,0:T(8,128)(2,1)}, u32[]{:S(2)}) copy-start(bf16[1,8,8,9,64]{4,2,3,1,0:T(8,128)(2,1)} %get-tuple-element.22) | copy-start | bytes 221188
  399.7 3.9 copy-start.6
Sparse Core Ops, SparseCore 0:
  113.9 285.7 all-reduce.2
where the time goes:
time: 419 us; the launch traced here: 412 us
  waiting for transfers between devices  286 us (68%)
  matrix products  47.8 us (11%)
  local copies, waits for them, and re-layouts  33.4 us (8%)
  starting transfers between devices  21.6 us (5%)
  between operations  14.7 us (4%)
  other arithmetic  8.16 us (2%)
    psum x1, waiting for transfers between devices, local(): lax.psum((grad_first, grad_down, grad_coarse), ('space', 'dp'))  285 us
    conv_general_dilated x3, matrix products, kernel_grad(): lax.conv_general_dilated(padded, grads, (1, 1, 1), 'VALID', rhs_dilation=...  38.8 us
    unnamed x39, local copies, waits for them, and re-layouts  16.7 us
    ppermute x3, starting transfers between devices, padded_2(): lax.ppermute(tail, axis, [(i, (i + 1) % count) for i in range(ends)])  13.1 us
    concatenate x6, local copies, waits for them, and re-layouts, padded_2(): jnp.concatenate([lax.ppermute(tail, axis, [(i, (i + 1) % count) for i in...  10.8 us
    ppermute x3, starting transfers between devices, padded_2(): lax.ppermute(head, axis, [((i + 1) % count, i) for i in range(ends)])  8.54 us
  transfers between devices with their start and end apart: 7, of which 2 were waited for; matrix products, arithmetic and copies ran while one was open for 5% of the time, Pallas kernels for 0%

commit v1 on v0

v1 whole, which is shorter than its diff:
```python
import jax
import jax.numpy as jnp
from jax import lax
from jax.experimental import pallas as pl
from jax.experimental.pallas import tpu as pltpu
from jax.sharding import PartitionSpec as P

F32, BF16 = jnp.float32, jnp.bfloat16
PARAMS = pltpu.CompilerParams(vmem_limit_bytes=48 * 1024 * 1024)
NN = (((1,), (0,)), ((), ()))
NT = (((1,), (1,)), ((), ()))


def dot(a, b, dims=NN):
    return lax.dot_general(a, b, dims, preferred_element_type=F32)


def low_lanes(shape):
    return lax.broadcasted_iota(jnp.int32, shape, 1) < 64


def pick_matrix():
    row = lax.broadcasted_iota(jnp.int32, (256, 128), 0)
    col = lax.broadcasted_iota(jnp.int32, (256, 128), 1)
    return (2 * (row % 64) - 1 + row // 64 == col).astype(F32).astype(BF16)


def twice():
    row = lax.broadcasted_iota(jnp.int32, (64, 128), 0)
    col = lax.broadcasted_iota(jnp.int32, (64, 128), 1)
    return (row == col % 64).astype(F32).astype(BF16)


def gather_taps(plane, out):
    picked = dot(pick_matrix(), plane, NT).astype(BF16)
    for y in range(8):
        for tz in range(4):
            out[y * 64 : y * 64 + 64, tz * 128 : tz * 128 + 128] = picked[
                tz * 64 : tz * 64 + 64, y * 128 : y * 128 + 128
            ]
    low = low_lanes((64, 128))
    zero = jnp.zeros((64, 128), BF16)
    for y in range(8):
        for tz in range(4):
            block = picked[tz * 64 : tz * 64 + 64]
            above = block[:, y * 128 - 128 : y * 128] if y > 0 else zero
            below = block[:, y * 128 + 128 : y * 128 + 256] if y < 7 else zero
            out[y * 64 : y * 64 + 64, 512 + tz * 128 : 640 + tz * 128] = jnp.where(
                low, below, above
            )


def gather_coarse(field, out):
    row = lax.broadcasted_iota(jnp.int32, (512, 128), 0) % 64
    low = low_lanes((512, 128))
    before = jnp.where(row == 0, 0.0, pltpu.roll(field, 1, 0))
    after = jnp.where(row == 63, 0.0, pltpu.roll(field, 511, 0))
    sides = jnp.where(low, before, after).astype(BF16)
    mid = field.astype(BF16)
    zero = jnp.zeros((64, 128), BF16)
    up = jnp.concatenate([zero, field[:448].astype(BF16)], 0)
    down = jnp.concatenate([field[64:].astype(BF16), zero], 0)
    out[0:64, 0:128] = zero
    out[64:512, 0:128] = sides[:448]
    out[:, 128:256] = sides
    out[0:448, 256:384] = sides[64:]
    out[448:512, 256:384] = zero
    out[:, 384:512] = jnp.where(low, up, down)
    out[:, 512:640] = mid


def prepare_kernel(own, w_first, w_down, w_coarse, cot, part, fw, dw, cw, bw, taps):
    low = low_lanes((64, 128))
    zero = jnp.zeros((64, 128), BF16)
    pair = twice()

    def both(ref, k):
        return dot(ref[k * 64 : k * 64 + 64], pair).astype(BF16)

    for dx in range(3):
        for tz in range(4):
            for qz in range(2):
                iz = tz - qz
                w = [both(w_first, dx * 9 + iy * 3 + iz) for iy in range(3)] if 0 <= iz < 3 else None
                for side in range(2):
                    at = side * 512 + tz * 128
                    lanes = slice(qz * 128, qz * 128 + 128)
                    if w is None:
                        first = second = zero
                    elif side == 0:
                        first = jnp.where(low, w[1], w[0])
                        second = jnp.where(low, w[2], w[1])
                    else:
                        first = jnp.where(low, zero, w[2])
                        second = jnp.where(low, w[0], zero)
                    fw[dx, at : at + 64, lanes] = first
                    fw[dx, at + 64 : at + 128, lanes] = second
    for x in range(2):
        for qz in range(2):
            for qy in range(2):
                k = x * 4 + qy * 2 + qz
                at = (x * 4 + qz * 2 + qy) * 64
                dw[at : at + 64] = both(w_down, k)
    order = [(0, 0), (0, 2), (1, 0), (1, 2), (2, 0), (2, 2), (0, 1), (2, 1), (1, 1), None]
    for dx in range(3):
        back = []
        for j, tap in enumerate(order):
            at = dx * 640 + j * 64
            if tap is None:
                cw[at : at + 64] = zero
                back.append(zero)
            else:
                cw[at : at + 64] = both(w_coarse, dx * 9 + tap[0] * 3 + tap[1])
                back.append(both(w_coarse, (2 - dx) * 9 + (2 - tap[0]) * 3 + 2 - tap[1]))
        for j in range(5):
            at = dx * 640 + j * 128
            bw[:, at : at + 128] = jnp.where(low, back[2 * j], back[2 * j + 1])
    for x in range(2):
        gather_taps(own[x * 1024 : x * 1024 + 1024], taps.at[x])
    part[0] = dot(taps[0], fw[1]) + dot(taps[1], fw[2])
    part[1] = dot(taps[0], fw[0]) + dot(taps[1], fw[1])


def first_kernel(before, after, part, fw, dw, act, slope, send, taps):
    low = low_lanes((256, 128))
    for x, side in enumerate((before, after)):
        gather_taps(side[0:1024], taps)
        pre = part[x] + dot(taps[...], fw[2 * x])
        s = jax.nn.sigmoid(pre)
        act[:, x * 256 : x * 256 + 256] = (pre * s).astype(BF16)
        slope[:, x * 256 : x * 256 + 256] = s * (1.0 + pre * (1.0 - s))
    down = dot(act[...], dw[...])
    send[...] = jnp.where(low, down[:256], down[256:]).astype(BF16)


def rest_kernel(
    d0, d1, d2, d3, d4, own, before, after, cot, act, slope, dw, cw, bw, out, grads, taps, near, near2
):
    low = low_lanes((64, 128))
    low2 = low_lanes((256, 128))
    pair = twice()
    for p, ref in enumerate((d0, d1, d2, d3, d4)):
        field = ref[...].astype(F32)
        turned = pltpu.roll(field, 64, 1)
        field = jnp.concatenate(
            [jnp.where(low2, field, turned), jnp.where(low2, turned, field)], 0
        )
        gather_coarse(field, near.at[p])
    mid = None
    for p in range(3):
        pre = dot(near[p], cw[0:640]) + dot(near[p + 1], cw[640:1280]) + dot(near[p + 2], cw[1280:1920])
        s = jax.nn.sigmoid(pre)
        if p == 1:
            silu = (pre * s).T
            out[...] = silu[0:64].astype(BF16)
        source = (before, cot, after)[p]
        base = 0 if p == 1 else 1024
        ct = jnp.concatenate(
            [
                source[base + j * 64 : base + j * 64 + 64].astype(F32).T.astype(BF16)
                for j in range(4)
            ],
            0,
        )
        grad = (dot(ct, pair) * (s * (1.0 + pre * (1.0 - s)))).astype(BF16).astype(F32)
        if p == 1:
            mid = grad
        gather_coarse(grad, near2.at[p])
    mid_t = mid.T[0:64].astype(BF16)
    center = []
    for dx in range(3):
        g = dot(mid_t, near[dx + 1])
        for j in range(4):
            at = (14 + dx * 4 + j) * 64
            grads[at : at + 64] = g[:, j * 128 : j * 128 + 128].astype(BF16)
        center.append(g[:, 512:640])
    grads[26 * 64 : 27 * 64] = jnp.where(low, center[0], center[1]).astype(BF16)
    grads[27 * 64 : 28 * 64] = center[2].astype(BF16)
    down_grad = (
        dot(near2[0], bw[:, 0:640], NT)
        + dot(near2[1], bw[:, 640:1280], NT)
        + dot(near2[2], bw[:, 1280:1920], NT)
    )
    dg = down_grad.astype(BF16)
    dg_t = down_grad.T.astype(BF16)
    gd = dot(dg_t, act[...])
    for j in range(4):
        at = (28 + j) * 64
        grads[at : at + 64] = gd[:, j * 128 : j * 128 + 128].astype(BF16)
    fg = dot(dg, dw[:, 0:64], NT) * slope[...]
    fg_t = fg.T.astype(BF16)
    for p, plane in enumerate((before[0:1024], own[0:1024], own[1024:2048], after[0:1024])):
        gather_taps(plane, taps.at[p])
    mids, zero_y = [], []
    for dx in range(3):
        g = dot(fg_t[0:256], taps[dx]) + dot(fg_t[256:512], taps[dx + 1])
        for iz in range(3):

            def summed(side, qy):
                at = side * 512 + iz * 128
                return (
                    g[qy * 64 : qy * 64 + 64, at : at + 128]
                    + g[128 + qy * 64 : 192 + qy * 64, at + 128 : at + 256]
                )

            z0, z1, u0, u1 = summed(0, 0), summed(0, 1), summed(1, 0), summed(1, 1)
            j = dx * 3 + iz
            grads[j * 64 : j * 64 + 64] = (
                z0 + pltpu.roll(jnp.where(low, u1, z1), 64, 1)
            ).astype(BF16)
            zero_y.append((z1, u0))
    zero_y.append((jnp.zeros((64, 128), F32),) * 2)
    for m in range(5):
        (z1a, u0a), (z1b, u0b) = zero_y[2 * m], zero_y[2 * m + 1]
        at = (9 + m) * 64
        grads[at : at + 64] = (
            jnp.where(low, z1a, u0b) + pltpu.roll(jnp.where(low, z1b, u0a), 64, 1)
        ).astype(BF16)


def unpack_kernel(packed, first, down, coarse):
    def block(b):
        return packed[b * 64 : b * 64 + 64].astype(F32).T

    for j in range(9):
        dx, iz = j // 3, j % 3
        t = block(j)
        first[dx, 1, iz] = t[0:64]
        first[dx, 2, iz] = t[64:128]
    for m in range(5):
        t = block(9 + m)
        for h in range(2):
            j = 2 * m + h
            if j < 9:
                first[j // 3, 0, j % 3] = t[h * 64 : h * 64 + 64]
    pairs = [((0, 0), (0, 2)), ((1, 0), (1, 2)), ((2, 0), (2, 2)), ((0, 1), (2, 1))]
    for dx in range(3):
        for j in range(4):
            t = block(14 + dx * 4 + j)
            for h in range(2):
                dy, dz = pairs[j][h]
                coarse[dx, dy, dz] = t[h * 64 : h * 64 + 64]
    t = block(26)
    coarse[0, 1, 1] = t[0:64]
    coarse[1, 1, 1] = t[64:128]
    coarse[2, 1, 1] = block(27)[0:64]
    for j in range(4):
        t = block(28 + j)
        for qy in range(2):
            down[j // 2, qy, j % 2] = t[qy * 64 : qy * 64 + 64]


def call(kernel, outs, scratch=()):
    return pl.pallas_call(
        kernel,
        out_shape=[jax.ShapeDtypeStruct(s, d) for s, d in outs],
        scratch_shapes=[pltpu.VMEM(s, d) for s, d in scratch],
        compiler_params=PARAMS,
    )


def swap(y, axis):
    return lax.all_to_all(y, axis, 0, 0, tiled=True)


def total(part):
    space, dp = lax.axis_size("space"), lax.axis_size("dp")
    rows = part.shape[0]
    y = swap(part.reshape(dp, rows // dp, 128), "dp")
    y = jnp.sum(y.astype(F32), 0).astype(BF16)
    y = swap(y.reshape(space, rows // dp // space, 128), "space")
    y = jnp.sum(y.astype(F32), 0).astype(BF16)
    y = swap(jnp.broadcast_to(y[None], (space,) + y.shape), "space").reshape(rows // dp, 128)
    return swap(jnp.broadcast_to(y[None], (dp,) + y.shape), "dp").reshape(rows, 128)


def local(volumes, w_first, w_down, w_coarse, cotangent):
    n = lax.axis_size("space")

    def shift(value, by):
        steps = [(i, i + by) for i in range(n) if 0 <= i + by < n]
        return lax.ppermute(value, "space", steps)

    own = jnp.transpose(volumes[0], (1, 2, 0, 3)).reshape(2048, 128)
    cot = jnp.transpose(cotangent.reshape(64, 4, 128), (1, 0, 2)).reshape(256, 128)
    before = shift(jnp.concatenate([own[1024:], cot]), 1)
    after = shift(jnp.concatenate([own[:1024], cot]), -1)
    part, fw, dw, cw, bw = call(
        prepare_kernel,
        [((2, 512, 256), F32), ((3, 1024, 256), BF16), ((512, 128), BF16), ((1920, 128), BF16), ((64, 1920), BF16)],
        [((2, 512, 1024), BF16)],
    )(own, w_first.reshape(1728, 64), w_down.reshape(512, 64), w_coarse.reshape(1728, 64), cot)
    act, slope, down = call(
        first_kernel,
        [((512, 512), BF16), ((512, 512), F32), ((256, 128), BF16)],
        [((512, 1024), BF16)],
    )(before, after, part, fw, dw)
    halo = [shift(down, 2), shift(down, 1), down, shift(down, -1), shift(down, -2)]
    out, grads = call(
        rest_kernel,
        [((64, 512), BF16), ((2048, 128), BF16)],
        [((4, 512, 1024), BF16), ((5, 512, 640), BF16), ((3, 512, 640), BF16)],
    )(*halo, own, before, after, cot, act, slope, dw, cw, bw)
    first, down_w, coarse = call(
        unpack_kernel,
        [((3, 3, 3, 64, 64), F32), ((2, 2, 2, 64, 64), F32), ((3, 3, 3, 64, 64), F32)],
    )(total(grads))
    return (out.reshape(1, 64, 1, 8, 64), first, down_w, coarse)


def solution(mesh):
    return jax.shard_map(
        local,
        mesh=mesh,
        in_specs=(
            P("dp", None, "space", None, None),
            P(),
            P(),
            P(),
            P("dp", None, "space", None, None),
        ),
        out_specs=(P("dp", None, "space", None, None), P(), P(), P()),
        check_vma=False,
    )
```

time: 419 us -> 117 us (0.28); the launches traced: 412 us -> 117 us
  waiting for transfers between devices: 286 us -> 18.6 us
  blocking collectives: 0 us -> 54.5 us
  matrix products: 47.8 us -> 0 us
  local copies, waits for them, and re-layouts: 33.4 us -> 4.24 us
  between operations: 14.7 us -> 0.85 us
  Pallas kernels: 0 us -> 11.1 us
  other arithmetic: 8.16 us -> 0.16 us
  starting transfers between devices: 21.6 us -> 27.1 us
    psum x1 -> x0, waiting for transfers between devices: 285 us -> none  [local(): lax.psum((grad_first, grad_down, grad_coarse), ('space', 'dp'))]
    all_to_all x0 -> x3, blocking collectives: none -> 54.5 us  [swap(): return lax.all_to_all(y, axis, 0, 0, tiled=True)]
    conv_general_dilated x7 -> x0, matrix products: 47.4 us -> none  [the longest x3 38.8 us: kernel_grad(): lax.conv_general_dilated(padded, grads, (1, 1, 1), 'VALID', rhs_dilation=...]
    unnamed x39 -> x8, local copies, waits for them, and re-layouts: 16.7 us -> 0.03 us
    all_to_all x0 -> x1, waiting for transfers between devices: none -> 15.8 us  [swap(): return lax.all_to_all(y, axis, 0, 0, tiled=True)]
    pallas_call x0 -> x4, Pallas kernels: none -> 11.1 us  [the longest x1 6.03 us: local(): call(rest_kernel, [((64, 512), BF16), ((2048, 128), BF16)], [((4, 512, 10...]
    concatenate x6 -> x0, local copies, waits for them, and re-layouts: 10.8 us -> none  [padded_2(): jnp.concatenate([lax.ppermute(tail, axis, [(i, (i + 1) % count) for i in...]
    convert_element_type x4 -> x0, other arithmetic: 4.56 us -> none  [the longest x2 2.78 us: local(): first_act = jax.nn.silu(first_pre).astype(jnp.bfloat16)]
  transfers between devices with their start and end apart: 7 -> 7, of which waited for: 2 -> 3; matrix products, arithmetic and copies ran while one was open for 5% -> 1% of each run, Pallas kernels for 0% -> 2%
where the time goes in v1:
time: 117 us
  blocking collectives  54.5 us (47%)
  starting transfers between devices  27.1 us (23%)
  waiting for transfers between devices  18.6 us (16%)
  Pallas kernels  11.1 us (9%)
  local copies, waits for them, and re-layouts  4.24 us (4%)
    all_to_all x3, blocking collectives, swap(): return lax.all_to_all(y, axis, 0, 0, tiled=True)  54.5 us
    ppermute x6, starting transfers between devices, shift(): return lax.ppermute(value, 'space', steps)  22.7 us
    all_to_all x1, waiting for transfers between devices, swap(): return lax.all_to_all(y, axis, 0, 0, tiled=True)  15.8 us
    pallas_call x1, Pallas kernels, local(): call(rest_kernel, [((64, 512), BF16), ((2048, 128), BF16)], [((4, 512, 10...  6.03 us
    all_to_all x1, starting transfers between devices, swap(): return lax.all_to_all(y, axis, 0, 0, tiled=True)  4.43 us
    ppermute x6, waiting for transfers between devices, shift(): return lax.ppermute(value, 'space', steps)  2.84 us
  transfers between devices with their start and end apart: 7, of which 3 were waited for; matrix products, arithmetic and copies ran while one was open for 1% of the time, Pallas kernels for 2%

profile of v1, /device:TPU:1, one launch (start us, length us, event | category | flops | bytes accessed | tf_op | source)
XLA Modules:
  0.0 116.6 jit_solution(15946344933346324555)
XLA Ops:
  0.6 1.0 reshape.42
  1.7 0.0 copy-start.3
  1.7 1.1 fusion
  2.8 0.0 copy-start
  2.8 0.0 copy-start.1
  2.8 0.0 copy-start.2
  2.9 0.1 copy.21
  2.9 0.1 copy.19
  3.1 8.9 %collective-permute-start.1 = (bf16[1280,128]{1,0:T(8,128)(2,1)S(1)}, bf16[1280,128]{1,0:T(8,128)(2,1)S(1)}, u32[]{:S(2)}, u32[]{:S(2)}) collective-permute-start(bf16[1280,128]{1,0:T(8,128)(2,1)S(1)} %get-tuple-element.44), channel_id=1, source_target_pairs={{32,0},{64,32},{96,64},{128,96},{160,128},{192,160},{224,192},{256... | collective-permute-start | bytes 983048 | tf_op jit(solution)/shard_map/ppermute | solution.py:282
  12.0 1.9 %collective-permute-start = (bf16[1280,128]{1,0:T(8,128)(2,1)S(1)}, bf16[1280,128]{1,0:T(8,128)(2,1)S(1)}, u32[]{:S(2)}, u32[]{:S(2)}) collective-permute-start(bf16[1280,128]{1,0:T(8,128)(2,1)S(1)} %get-tuple-element.45), channel_id=1, source_target_pairs={{0,32},{32,64},{64,96},{96,128},{128,160},{160,192},{192,224},{224... | collective-permute-start | bytes 983048 | tf_op jit(solution)/shard_map/ppermute | solution.py:282
  13.9 0.0 copy-done.3
  13.9 0.2 copy.22
  14.1 0.0 copy-done
  14.2 0.0 copy-done.1
  14.2 0.0 copy-done.2
  14.2 2.2 %shard_map.84 = (f32[2,512,256]{2,1,0:T(8,128)S(1)}, bf16[3,1024,256]{2,1,0:T(8,128)(2,1)S(1)}, bf16[512,128]{1,0:T(8,128)(2,1)S(1)}, bf16[1920,128]{1,0:T(8,128)(2,1)S(1)}, bf16[64,1920]{1,0:T(8,128)(2,1)S(1)}) custom-call(bf16[2048,128]{1,0:T(8,128)(2,1)S(1)} %bitcast.19, bf16[1728,64]{1,0:T(8,128)(2,1)S(1)} %bitcast.26, bf16[512,64]{1,0:T(8,128)(2,1)S(1)} %bitcast.28, ...), custom_call_target="tpu_custom_call" | custom-call | tf_op jit(solution)/shard_map/pallas_call | solution.py:288
  16.4 0.0 collective-permute-done.1.after
  16.4 1.5 %collective-permute-done.before = bf16[1280,128]{1,0:T(8,128)(2,1)S(1)} collective-permute-done((bf16[1280,128]{1,0:T(8,128)(2,1)S(1)}, bf16[1280,128]{1,0:T(8,128)(2,1)S(1)}, u32[]{:S(2)}, u32[]{:S(2)}) %collective-permute-start) | collective-permute-done | bytes 327712 | tf_op jit(solution)/shard_map/ppermute | solution.py:282
  17.9 1.4 %shard_map.85 = (bf16[512,512]{1,0:T(8,128)(2,1)S(1)}, f32[512,512]{1,0:T(8,128)S(1)}, bf16[256,128]{1,0:T(8,128)(2,1)S(1)}) custom-call(bf16[1280,128]{1,0:T(8,128)(2,1)S(1)} %collective-permute-done.before, bf16[1280,128]{1,0:T(8,128)(2,1)S(1)} %collective-permute-done.1.after, f32[2,512,256]{2,1,0:T(8,128)S(1)} %get-tuple-element.17.part, ...), custom_call_target="tpu_custom_call" | custom-call | tf_op jit(solution)/shard_map/pallas_call | solution.py:293
  19.3 1.3 %collective-permute-start.5 = (bf16[256,128]{1,0:T(8,128)(2,1)S(1)}, bf16[256,128]{1,0:T(8,128)(2,1)S(1)}, u32[]{:S(2)}, u32[]{:S(2)}) collective-permute-start(bf16[256,128]{1,0:T(8,128)(2,1)S(1)} %get-tuple-element.20.d2), channel_id=1, source_target_pairs={{64,0},{96,32},{128,64},{160,96},{192,128},{224,160},{256,192},{28... | collective-permute-start | bytes 196616 | tf_op jit(solution)/shard_map/ppermute | solution.py:282
  20.6 1.9 %collective-permute-start.4 = (bf16[256,128]{1,0:T(8,128)(2,1)S(1)}, bf16[256,128]{1,0:T(8,128)(2,1)S(1)}, u32[]{:S(2)}, u32[]{:S(2)}) collective-permute-start(bf16[256,128]{1,0:T(8,128)(2,1)S(1)} %get-tuple-element.20.d2), channel_id=1, source_target_pairs={{32,0},{64,32},{96,64},{128,96},{160,128},{192,160},{224,192},{256... | collective-permute-start | bytes 196616 | tf_op jit(solution)/shard_map/ppermute | solution.py:282
  22.5 5.0 %collective-permute-start.3 = (bf16[256,128]{1,0:T(8,128)(2,1)S(1)}, bf16[256,128]{1,0:T(8,128)(2,1)S(1)}, u32[]{:S(2)}, u32[]{:S(2)}) collective-permute-start(bf16[256,128]{1,0:T(8,128)(2,1)S(1)} %get-tuple-element.20.d2), channel_id=1, source_target_pairs={{0,32},{32,64},{64,96},{96,128},{128,160},{160,192},{192,224},{224... | collective-permute-start | bytes 196616 | tf_op jit(solution)/shard_map/ppermute | solution.py:282
  27.5 3.6 %collective-permute-start.2 = (bf16[256,128]{1,0:T(8,128)(2,1)S(1)}, bf16[256,128]{1,0:T(8,128)(2,1)S(1)}, u32[]{:S(2)}, u32[]{:S(2)}) collective-permute-start(bf16[256,128]{1,0:T(8,128)(2,1)S(1)} %get-tuple-element.20.d2), channel_id=1, source_target_pairs={{0,64},{32,96},{64,128},{96,160},{128,192},{160,224},{192,256},{22... | collective-permute-start | bytes 196616 | tf_op jit(solution)/shard_map/ppermute | solution.py:282
  31.2 0.0 collective-permute-done.5.d4
  31.2 0.0 collective-permute-done.4.d3
  31.2 0.0 collective-permute-done.3.d1
  31.2 1.3 %collective-permute-done.2.d0 = bf16[256,128]{1,0:T(8,128)(2,1)S(1)} collective-permute-done((bf16[256,128]{1,0:T(8,128)(2,1)S(1)}, bf16[256,128]{1,0:T(8,128)(2,1)S(1)}, u32[]{:S(2)}, u32[]{:S(2)}) %collective-permute-start.2) | collective-permute-done | bytes 65568 | tf_op jit(solution)/shard_map/ppermute | solution.py:282
  32.5 6.0 %shard_map.86 = (bf16[64,512]{1,0:T(8,128)(2,1)S(1)}, bf16[2048,128]{1,0:T(8,128)(2,1)S(1)}) custom-call(bf16[256,128]{1,0:T(8,128)(2,1)S(1)} %collective-permute-done.2.d0, bf16[256,128]{1,0:T(8,128)(2,1)S(1)} %collective-permute-done.3.d1, bf16[256,128]{1,0:T(8,128)(2,1)S(1)} %get-tuple-element.20.d2, bf16[256,128]{1,0:T(8,128)(2,1)S(1)} %collective-permute-done.4.d3, ...), custom_call_target="tpu_custom_call" | custom-call | tf_op jit(solution)/shard_map/pallas_call | solution.py:299
  38.5 23.8 %all_to_all.20 = bf16[32,64,128]{2,1,0:T(8,128)(2,1)S(1)} all-to-all(bf16[32,64,128]{2,1,0:T(8,128)(2,1)S(1)} %bitcast.25), channel_id=1, replica_groups=mesh['space'=16,'dp'=32] {'dp'}, dimensions={0} | all-to-all | bytes 1048576 | tf_op jit(solution)/shard_map/all_to_all | solution.py:263
  62.3 0.1 reduce_sum.24
  62.4 20.5 %all_to_all.21 = bf16[16,4,128]{2,1,0:T(4,128)(2,1)S(1)} all-to-all(bf16[16,4,128]{2,1,0:T(4,128)(2,1)S(1)} %bitcast.34), channel_id=1, replica_groups=mesh['space'=16,'dp'=32] {'space'}, dimensions={0} | all-to-all | bytes 32768 | tf_op jit(solution)/shard_map/all_to_all | solution.py:263
  83.0 10.2 %all_to_all.22 = bf16[16,4,128]{2,1,0:T(4,128)(2,1)S(1)} all-to-all(bf16[16,4,128]{2,1,0:T(4,128)(2,1)S(1)} %broadcast_in_dim.6), channel_id=1, replica_groups=mesh['space'=16,'dp'=32] {'space'}, dimensions={0} | all-to-all | bytes 32768 | tf_op jit(solution)/shard_map/all_to_all | solution.py:263
  93.1 0.9 broadcast_in_dim.15
  94.1 4.4 %all-to-all-start.3 = ((bf16[32,64,128]{2,1,0:T(8,128)(2,1)}), bf16[32,64,128]{2,1,0:T(8,128)(2,1)S(1)}, u32[]{:S(2)}, u32[]{:S(2)}) async-start(bf16[32,64,128]{2,1,0:T(8,128)(2,1)} %broadcast_in_dim.15), calls=%async_computation.3 | async-start | bytes 1048576 | tf_op jit(solution)/shard_map/all_to_all | solution.py:263
  98.5 0.8 reshape.48
  99.3 15.8 %all-to-all-done.3 = bf16[32,64,128]{2,1,0:T(8,128)(2,1)S(1)} async-done(((bf16[32,64,128]{2,1,0:T(8,128)(2,1)}), bf16[32,64,128]{2,1,0:T(8,128)(2,1)S(1)}, u32[]{:S(2)}, u32[]{:S(2)}) %all-to-all-start.3) | async-done | bytes 524320 | tf_op jit(solution)/shard_map/all_to_all | solution.py:263
  115.1 1.5 %shard_map.87 = (f32[3,3,3,64,64]{4,3,2,1,0:T(8,128)}, f32[2,2,2,64,64]{4,3,2,1,0:T(8,128)}, f32[3,3,3,64,64]{4,3,2,1,0:T(8,128)}) custom-call(bf16[2048,128]{1,0:T(8,128)(2,1)S(1)} %bitcast.21), custom_call_target="tpu_custom_call" | custom-call | tf_op jit(solution)/shard_map/pallas_call | solution.py:304
  (4 shorter events, 0.1 us)
Async XLA Ops:
  1.7 12.2 %copy-start.3 = (bf16[1,64,2,16,128]{4,3,2,1,0:T(8,128)(2,1)S(1)}, bf16[1,64,2,16,128]{4,3,2,1,0:T(8,128)(2,1)}, u32[]{:S(2)}) copy-start(bf16[1,64,2,16,128]{4,3,2,1,0:T(8,128)(2,1)} %param.5) | copy-start | bytes 1572868
  2.8 11.3 %copy-start = (bf16[3,3,3,64,64]{4,3,2,1,0:T(8,128)(2,1)S(1)}, bf16[3,3,3,64,64]{4,3,2,1,0:T(8,128)(2,1)}, u32[]{:S(2)}) copy-start(bf16[3,3,3,64,64]{4,3,2,1,0:T(8,128)(2,1)} %param.6) | copy-start | bytes 663556
  2.8 11.3 %copy-start.1 = (bf16[3,3,3,64,64]{4,3,2,1,0:T(8,128)(2,1)S(1)}, bf16[3,3,3,64,64]{4,3,2,1,0:T(8,128)(2,1)}, u32[]{:S(2)}) copy-start(bf16[3,3,3,64,64]{4,3,2,1,0:T(8,128)(2,1)} %param.8) | copy-start | bytes 663556
  2.8 11.3 %copy-start.2 = (bf16[2,2,2,64,64]{4,3,2,1,0:T(8,128)(2,1)S(1)}, bf16[2,2,2,64,64]{4,3,2,1,0:T(8,128)(2,1)}, u32[]{:S(2)}) copy-start(bf16[2,2,2,64,64]{4,3,2,1,0:T(8,128)(2,1)} %param.7) | copy-start | bytes 196612
  3.1 13.3 %collective-permute-start.1 = (bf16[1280,128]{1,0:T(8,128)(2,1)S(1)}, bf16[1280,128]{1,0:T(8,128)(2,1)S(1)}, u32[]{:S(2)}, u32[]{:S(2)}) collective-permute-start(bf16[1280,128]{1,0:T(8,128)(2,1)S(1)} %get-tuple-element.44), channel_id=1, source_target_pairs={{32,0},{64,32},{96,64},{128,96},{160,128},{192,160},{224,192},{256... | collective-permute-start | bytes 983048 | tf_op jit(solution)/shard_map/ppermute | solution.py:282
  12.0 5.9 %collective-permute-start = (bf16[1280,128]{1,0:T(8,128)(2,1)S(1)}, bf16[1280,128]{1,0:T(8,128)(2,1)S(1)}, u32[]{:S(2)}, u32[]{:S(2)}) collective-permute-start(bf16[1280,128]{1,0:T(8,128)(2,1)S(1)} %get-tuple-element.45), channel_id=1, source_target_pairs={{0,32},{32,64},{64,96},{96,128},{128,160},{160,192},{192,224},{224... | collective-permute-start | bytes 983048 | tf_op jit(solution)/shard_map/ppermute | solution.py:282
  19.3 11.9 %collective-permute-start.5 = (bf16[256,128]{1,0:T(8,128)(2,1)S(1)}, bf16[256,128]{1,0:T(8,128)(2,1)S(1)}, u32[]{:S(2)}, u32[]{:S(2)}) collective-permute-start(bf16[256,128]{1,0:T(8,128)(2,1)S(1)} %get-tuple-element.20.d2), channel_id=1, source_target_pairs={{64,0},{96,32},{128,64},{160,96},{192,128},{224,160},{256,192},{28... | collective-permute-start | bytes 196616 | tf_op jit(solution)/shard_map/ppermute | solution.py:282
  20.6 10.6 %collective-permute-start.4 = (bf16[256,128]{1,0:T(8,128)(2,1)S(1)}, bf16[256,128]{1,0:T(8,128)(2,1)S(1)}, u32[]{:S(2)}, u32[]{:S(2)}) collective-permute-start(bf16[256,128]{1,0:T(8,128)(2,1)S(1)} %get-tuple-element.20.d2), channel_id=1, source_target_pairs={{32,0},{64,32},{96,64},{128,96},{160,128},{192,160},{224,192},{256... | collective-permute-start | bytes 196616 | tf_op jit(solution)/shard_map/ppermute | solution.py:282
  22.5 8.7 %collective-permute-start.3 = (bf16[256,128]{1,0:T(8,128)(2,1)S(1)}, bf16[256,128]{1,0:T(8,128)(2,1)S(1)}, u32[]{:S(2)}, u32[]{:S(2)}) collective-permute-start(bf16[256,128]{1,0:T(8,128)(2,1)S(1)} %get-tuple-element.20.d2), channel_id=1, source_target_pairs={{0,32},{32,64},{64,96},{96,128},{128,160},{160,192},{192,224},{224... | collective-permute-start | bytes 196616 | tf_op jit(solution)/shard_map/ppermute | solution.py:282
  27.5 5.0 %collective-permute-start.2 = (bf16[256,128]{1,0:T(8,128)(2,1)S(1)}, bf16[256,128]{1,0:T(8,128)(2,1)S(1)}, u32[]{:S(2)}, u32[]{:S(2)}) collective-permute-start(bf16[256,128]{1,0:T(8,128)(2,1)S(1)} %get-tuple-element.20.d2), channel_id=1, source_target_pairs={{0,64},{32,96},{64,128},{96,160},{128,192},{160,224},{192,256},{22... | collective-permute-start | bytes 196616 | tf_op jit(solution)/shard_map/ppermute | solution.py:282
  94.1 21.0 %all-to-all-start.3 = ((bf16[32,64,128]{2,1,0:T(8,128)(2,1)}), bf16[32,64,128]{2,1,0:T(8,128)(2,1)S(1)}, u32[]{:S(2)}, u32[]{:S(2)}) async-start(bf16[32,64,128]{2,1,0:T(8,128)(2,1)} %broadcast_in_dim.15), calls=%async_computation.3 | async-start | bytes 1048576 | tf_op jit(solution)/shard_map/all_to_all | solution.py:263

commit v2 on v1

v2 whole, which is shorter than its diff:
```python
import jax
import jax.numpy as jnp
from jax import lax
from jax.experimental import pallas as pl
from jax.experimental.pallas import tpu as pltpu
from jax.sharding import PartitionSpec as P

F32, BF16 = jnp.float32, jnp.bfloat16
PARAMS = pltpu.CompilerParams(vmem_limit_bytes=32 * 1024 * 1024)
NN = (((1,), (0,)), ((), ()))
NT = (((1,), (1,)), ((), ()))


def dot(a, b, dims=NN):
    return lax.dot_general(a, b, dims, preferred_element_type=F32)


def low_lanes(shape):
    return lax.broadcasted_iota(jnp.int32, shape, 1) < 64


def pick_matrix():
    row = lax.broadcasted_iota(jnp.int32, (256, 128), 0)
    col = lax.broadcasted_iota(jnp.int32, (256, 128), 1)
    return (2 * (row % 64) - 1 + row // 64 == col).astype(F32).astype(BF16)


def twice():
    row = lax.broadcasted_iota(jnp.int32, (64, 128), 0)
    col = lax.broadcasted_iota(jnp.int32, (64, 128), 1)
    return (row == col % 64).astype(F32).astype(BF16)


def gather_taps(plane, out):
    picked = dot(pick_matrix(), plane, NT).astype(BF16)
    low = low_lanes((64, 128))
    zero = jnp.zeros((64, 128), BF16)
    for y in range(8):
        for tz in range(4):
            block = picked[tz * 64 : tz * 64 + 64]
            above = block[:, y * 128 - 128 : y * 128] if y > 0 else zero
            below = block[:, y * 128 + 128 : y * 128 + 256] if y < 7 else zero
            rows = slice(y * 64, y * 64 + 64)
            out[rows, tz * 128 : tz * 128 + 128] = block[:, y * 128 : y * 128 + 128]
            out[rows, 512 + tz * 128 : 640 + tz * 128] = jnp.where(low, below, above)


def gather_coarse(field, out):
    row = lax.broadcasted_iota(jnp.int32, (512, 128), 0) % 64
    low = low_lanes((512, 128))
    before = jnp.where(row == 0, 0.0, pltpu.roll(field, 1, 0))
    after = jnp.where(row == 63, 0.0, pltpu.roll(field, 511, 0))
    sides = jnp.where(low, before, after).astype(BF16)
    mid = field.astype(BF16)
    zero = jnp.zeros((64, 128), BF16)
    up = jnp.concatenate([zero, mid[:448]], 0)
    down = jnp.concatenate([mid[64:], zero], 0)
    out[0:64, 0:128] = zero
    out[64:512, 0:128] = sides[:448]
    out[:, 128:256] = sides
    out[0:448, 256:384] = sides[64:]
    out[448:512, 256:384] = zero
    out[:, 384:512] = jnp.where(low, up, down)
    out[:, 512:640] = mid


def turned(ref):
    field = ref.astype(F32)
    return field, pltpu.roll(field, 64, 1)


def doubled(ref):
    field, swapped = turned(ref)
    low = low_lanes((256, 128))
    return jnp.concatenate([jnp.where(low, field, swapped), jnp.where(low, swapped, field)], 0)


def edges_kernel(volumes, cot, first, last, planes, rows):
    for x, out in enumerate((first, last)):
        planes[x] = volumes[:, x].astype(F32).reshape(1024, 128)
        for y in range(16):
            out[y * 64 : y * 64 + 64] = planes[x, pl.ds(y, 64, stride=16), :].astype(BF16)
    rows[...] = cot[...].astype(F32).reshape(512, 64)
    for j in range(4):
        both = jnp.concatenate(
            [rows[pl.ds(j, 64, stride=8), :], rows[pl.ds(j + 4, 64, stride=8), :]], 0
        )
        block = both.T.astype(BF16)
        for out in (first, last):
            out[1024 + j * 64 : 1088 + j * 64] = block


def prepare_kernel(first, last, w_first, w_down, w_coarse, part, fw, dw, cw, bw, taps):
    low = low_lanes((64, 128))
    zero = jnp.zeros((64, 128), BF16)
    pair = twice()

    def both(ref, k):
        return dot(ref[k * 64 : k * 64 + 64], pair).astype(BF16)

    for dx in range(3):
        for tz in range(4):
            for qz in range(2):
                iz = tz - qz
                w = [both(w_first, dx * 9 + iy * 3 + iz) for iy in range(3)] if 0 <= iz < 3 else None
                for side in range(2):
                    at = dx * 1024 + side * 512 + tz * 128
                    lanes = slice(qz * 128, qz * 128 + 128)
                    if w is None:
                        upper = lower = zero
                    elif side == 0:
                        upper = jnp.where(low, w[1], w[0])
                        lower = jnp.where(low, w[2], w[1])
                    else:
                        upper = jnp.where(low, zero, w[2])
                        lower = jnp.where(low, w[0], zero)
                    fw[at : at + 64, lanes] = upper
                    fw[at + 64 : at + 128, lanes] = lower
    for x in range(2):
        for qz in range(2):
            for qy in range(2):
                k = x * 4 + qy * 2 + qz
                at = (x * 4 + qz * 2 + qy) * 64
                dw[at : at + 64] = both(w_down, k)
    order = [(0, 0), (0, 2), (1, 0), (1, 2), (2, 0), (2, 2), (0, 1), (2, 1), (1, 1), None]
    for j, tap in enumerate(order):
        if tap is None:
            w = [zero] * 3
        else:
            w = [both(w_coarse, dx * 9 + tap[0] * 3 + tap[1]) for dx in range(3)]
        w = [zero] * 2 + w + [zero] * 2
        for p in range(5):
            at = p * 640 + j * 64
            cw[at : at + 64, 0:128] = jnp.where(low, w[p + 2], w[p + 1])
            cw[at : at + 64, 128:256] = jnp.where(low, w[p], zero)
    for dx in range(3):
        back = [
            zero if tap is None else both(w_coarse, (2 - dx) * 9 + (2 - tap[0]) * 3 + 2 - tap[1])
            for tap in order
        ]
        for j in range(5):
            at = dx * 640 + j * 128
            bw[:, at : at + 128] = jnp.where(low, back[2 * j], back[2 * j + 1])
    for x, ref in enumerate((first, last)):
        gather_taps(ref[0:1024], taps.at[:, x * 1024 : x * 1024 + 1024])
    for x in range(2):
        part[x * 512 : x * 512 + 512] = dot(taps[...], fw[1024 - x * 1024 : 3072 - x * 1024])


def first_kernel(before, after, part, fw, dw, act, pre, send, taps):
    low = low_lanes((256, 128))
    for x, side in enumerate((before, after)):
        gather_taps(side[0:1024], taps)
        value = part[x * 512 : x * 512 + 512] + dot(taps[...], fw[x * 2048 : x * 2048 + 1024])
        pre[x * 512 : x * 512 + 512] = value
        act[:, x * 256 : x * 256 + 256] = (value * jax.nn.sigmoid(value)).astype(BF16)
    down = dot(act[...], dw[...])
    send[...] = jnp.where(low, down[:256], down[256:]).astype(BF16)


def beside_kernel(first, last, before, after, pre, down, cw, taps, slope, ct, own, acc):
    value = pre[...]
    s = jax.nn.sigmoid(value)
    slope[...] = s * (1.0 + value * (1.0 - s))
    for p, ref in enumerate((before, first, last, after)):
        gather_taps(ref[0:1024], taps.at[p * 512 : p * 512 + 512])
    low = low_lanes((256, 128))
    f0, t0 = turned(before[1024:1280])
    f1, t1 = turned(first[1024:1280])
    f2, t2 = turned(after[1024:1280])
    ct[0:256, 0:128] = jnp.where(low, f0, t1)
    ct[256:512, 0:128] = jnp.where(low, t0, f1)
    ct[0:256, 128:256] = f2
    ct[256:512, 128:256] = t2
    gather_coarse(doubled(down[...]), own)
    acc[...] = dot(own[...], cw[1280:1920])


def rest_kernel(
    core, d0, d1, d3, d4, act, slope, taps, ct, own, acc, dw, cw, bw, out, keep, send, grads, below, above, near
):
    low = low_lanes((64, 128))
    for p, ref in enumerate((d0, d1)):
        gather_coarse(doubled(ref[...]), below.at[:, p * 640 : p * 640 + 640])
    for p, ref in enumerate((d3, d4)):
        gather_coarse(doubled(ref[...]), above.at[:, p * 640 : p * 640 + 640])
    pre = acc[...] + dot(below[...], cw[0:1280]) + dot(above[...], cw[1920:3200])
    s = jax.nn.sigmoid(pre)
    out[...] = (pre[:, 0:128] * s[:, 0:128]).T[64:128].astype(BF16)
    grad = (ct[...] * (s * (1.0 + pre * (1.0 - s)))).astype(BF16).astype(F32)
    two, one = grad[:, 0:128], grad[:, 128:256]
    two_t, one_t = pltpu.roll(two, 64, 1), pltpu.roll(one, 64, 1)
    low2 = low_lanes((512, 128))
    gather_coarse(jnp.where(low2, two, two_t), near.at[:, 0:640])
    gather_coarse(jnp.where(low2, two_t, two), near.at[:, 640:1280])
    gather_coarse(jnp.where(low2, one, one_t), near.at[:, 1280:1920])
    dg_wide = dot(near[...], bw[...], NT)
    dg = dg_wide.astype(BF16)
    up = dot(dg, dw[:, 0:64], NT)
    fg_t = jnp.concatenate(
        [
            (up[:, x * 256 : x * 256 + 256] * slope[x * 512 : x * 512 + 512]).T.astype(BF16)
            for x in range(2)
        ],
        1,
    )
    mid_t = two.T[64:128].astype(BF16)
    center = []
    for dx, planes in enumerate((below[:, 640:1280], own[...], above[:, 0:640])):
        g = dot(mid_t, planes)
        for j in range(4):
            at = (14 + dx * 4 + j) * 64
            grads[at : at + 64] = g[:, j * 128 : j * 128 + 128].astype(BF16)
        center.append(g[:, 512:640])
    grads[26 * 64 : 27 * 64] = jnp.where(low, center[0], center[1]).astype(BF16)
    grads[27 * 64 : 28 * 64] = center[2].astype(BF16)
    gd = dot(dg_wide.T.astype(BF16), act[...])
    for j in range(4):
        at = (28 + j) * 64
        grads[at : at + 64] = gd[:, j * 128 : j * 128 + 128].astype(BF16)
    zero_y = []
    for dx in range(3):
        g = dot(fg_t, taps[dx * 512 : dx * 512 + 1024])
        for iz in range(3):

            def summed(side, qy):
                at = side * 512 + iz * 128
                return (
                    g[qy * 64 : qy * 64 + 64, at : at + 128]
                    + g[128 + qy * 64 : 192 + qy * 64, at + 128 : at + 256]
                )

            z0, z1, u0, u1 = summed(0, 0), summed(0, 1), summed(1, 0), summed(1, 1)
            j = dx * 3 + iz
            grads[j * 64 : j * 64 + 64] = (
                z0 + pltpu.roll(jnp.where(low, u1, z1), 64, 1)
            ).astype(BF16)
            zero_y.append((z1, u0))
    zero_y.append((jnp.zeros((64, 128), F32),) * 2)
    for m in range(5):
        (z1a, u0a), (z1b, u0b) = zero_y[2 * m], zero_y[2 * m + 1]
        at = (9 + m) * 64
        grads[at : at + 64] = (
            jnp.where(low, z1a, u0b) + pltpu.roll(jnp.where(low, z1b, u0a), 64, 1)
        ).astype(BF16)
    here = pl.multiple_of(core[0] * 1024, 1024)
    keep[...] = grads[pl.ds(here, 1024), :]
    send[...] = grads[pl.ds(pl.multiple_of(1024 - here, 1024), 1024), :]


def unpack_kernel(core, mine, other, first, down, coarse, packed):
    here = pl.multiple_of(core[0] * 1024, 1024)
    packed[pl.ds(here, 1024), :] = mine[...]
    packed[pl.ds(pl.multiple_of(1024 - here, 1024), 1024), :] = other[...]

    def block(b):
        return packed[b * 64 : b * 64 + 64].astype(F32).T

    for j in range(9):
        dx, iz = j // 3, j % 3
        t = block(j)
        first[dx, 1, iz] = t[0:64]
        first[dx, 2, iz] = t[64:128]
    for m in range(5):
        t = block(9 + m)
        for h in range(2):
            j = 2 * m + h
            if j < 9:
                first[j // 3, 0, j % 3] = t[h * 64 : h * 64 + 64]
    pairs = [((0, 0), (0, 2)), ((1, 0), (1, 2)), ((2, 0), (2, 2)), ((0, 1), (2, 1))]
    for dx in range(3):
        for j in range(4):
            t = block(14 + dx * 4 + j)
            for h in range(2):
                dy, dz = pairs[j][h]
                coarse[dx, dy, dz] = t[h * 64 : h * 64 + 64]
    t = block(26)
    coarse[0, 1, 1] = t[0:64]
    coarse[1, 1, 1] = t[64:128]
    coarse[2, 1, 1] = block(27)[0:64]
    for j in range(4):
        t = block(28 + j)
        for qy in range(2):
            down[j // 2, qy, j % 2] = t[qy * 64 : qy * 64 + 64]


def call(kernel, outs, scratch=(), scalars=0):
    specs = {}
    if scalars:
        specs["in_specs"] = [pl.BlockSpec(memory_space=pltpu.SMEM)] + [
            pl.BlockSpec(memory_space=pltpu.VMEM)
        ] * (scalars - 1)
    return pl.pallas_call(
        kernel,
        out_shape=[jax.ShapeDtypeStruct(s, d) for s, d in outs],
        scratch_shapes=[pltpu.VMEM(s, d) for s, d in scratch],
        compiler_params=PARAMS,
        **specs,
    )


def scatter_sum(y, axis, count, groups=None):
    y = y.reshape(count, y.shape[0] // count, 128)
    y = lax.all_to_all(y, axis, 0, 0, tiled=True, axis_index_groups=groups)
    return jnp.sum(y.astype(F32), 0).astype(BF16)


def spread(y, axis, count, groups=None):
    y = jnp.broadcast_to(y[None], (count,) + y.shape)
    return lax.all_to_all(y, axis, 0, 0, tiled=True, axis_index_groups=groups)


def local(volumes, w_first, w_down, w_coarse, cotangent):
    n, m = lax.axis_size("space"), lax.axis_size("dp")

    def shift(value, by):
        steps = [(i, i + by) for i in range(n) if 0 <= i + by < n]
        return lax.ppermute(value, "space", steps)

    def partner(value):
        return lax.ppermute(value, "space", [(i, i ^ 1) for i in range(n)])

    first, last = call(
        edges_kernel,
        [((1280, 128), BF16)] * 2,
        [((2, 1024, 128), F32), ((512, 64), F32)],
    )(volumes.reshape(64, 2, 16, 128), cotangent.reshape(64, 8, 64))
    before = shift(last, 1)
    after = shift(first, -1)
    part, fw, dw, cw, bw = call(
        prepare_kernel,
        [((1024, 256), F32), ((3072, 256), BF16), ((512, 128), BF16), ((3200, 256), BF16), ((64, 1920), BF16)],
        [((512, 2048), BF16)],
    )(first, last, w_first.reshape(1728, 64), w_down.reshape(512, 64), w_coarse.reshape(1728, 64))
    act, pre, down = call(
        first_kernel,
        [((512, 512), BF16), ((1024, 256), F32), ((256, 128), BF16)],
        [((512, 1024), BF16)],
    )(before, after, part, fw, dw)
    halo = [shift(down, 2), shift(down, 1), shift(down, -1), shift(down, -2)]
    taps, slope, ct, own, acc = call(
        beside_kernel,
        [((2048, 1024), BF16), ((1024, 256), F32), ((512, 256), F32), ((512, 640), BF16), ((512, 256), F32)],
    )(first, last, before, after, pre, down, cw)
    core = lax.rem(lax.axis_index("space"), 2).reshape(1)
    out, keep, send = call(
        rest_kernel,
        [((64, 512), BF16), ((1024, 128), BF16), ((1024, 128), BF16)],
        [((2048, 128), BF16), ((512, 1280), BF16), ((512, 1280), BF16), ((512, 1920), BF16)],
        scalars=14,
    )(core, *halo, act, slope, taps, ct, own, acc, dw, cw, bw)
    half = (keep.astype(F32) + partner(send).astype(F32)).astype(BF16)
    chips = [list(range(c, n, 2)) for c in range(2)]
    piece = scatter_sum(half, "dp", m)
    piece = jnp.sum(spread(piece, "space", n // 2, chips).astype(F32), 0).astype(BF16)
    mine = spread(piece, "dp", m).reshape(1024, 128)
    grad_first, grad_down, grad_coarse = call(
        unpack_kernel,
        [((3, 3, 3, 64, 64), F32), ((2, 2, 2, 64, 64), F32), ((3, 3, 3, 64, 64), F32)],
        [((2048, 128), BF16)],
        scalars=3,
    )(core, mine, partner(mine))
    return (out.reshape(1, 64, 1, 8, 64), grad_first, grad_down, grad_coarse)


def solution(mesh):
    return jax.shard_map(
        local,
        mesh=mesh,
        in_specs=(
            P("dp", None, "space", None, None),
            P(),
            P(),
            P(),
            P("dp", None, "space", None, None),
        ),
        out_specs=(P("dp", None, "space", None, None), P(), P(), P()),
        check_vma=False,
    )
```

time: 117 us -> 109 us (0.932)
  waiting for transfers between devices: 18.6 us -> 3.21 us
  local copies, waits for them, and re-layouts: 4.24 us -> 8.7 us
  Pallas kernels: 11.1 us -> 15.3 us
    all_to_all x1 -> x0, waiting for transfers between devices: 15.8 us -> none  [swap(): return lax.all_to_all(y, axis, 0, 0, tiled=True)]
    ppermute x0 -> x2, starting transfers between devices: none -> 8.27 us  [partner(): return lax.ppermute(value, 'space', [(i, i ^ 1) for i in range(n)])]
    unnamed x8 -> x18, local copies, waits for them, and re-layouts: 0.03 us -> 7.86 us
    all_to_all x1 -> x0, starting transfers between devices: 4.43 us -> none  [swap(): return lax.all_to_all(y, axis, 0, 0, tiled=True)]
    ppermute x6, starting transfers between devices: 22.7 us -> 18.4 us  [shift(): return lax.ppermute(value, 'space', steps)]
    pallas_call x3 -> x5, Pallas kernels: 9.57 us -> 13.7 us  [the longest x1 6.53 us: local(): call(rest_kernel, [((64, 512), BF16), ((1024, 128), BF16), ((1024, 128),...]
    ppermute x0 -> x2, waiting for transfers between devices: none -> 1.49 us  [partner(): return lax.ppermute(value, 'space', [(i, i ^ 1) for i in range(n)])]
    slice x3 -> x0, local copies, waits for them, and re-layouts: 1.26 us -> none  [the longest x2 1.2 us: local(): after = shift(jnp.concatenate([own[:1024], cot]), -1)]
  transfers between devices with their start and end apart: 7 -> 8, of which waited for: 3 -> 3; matrix products, arithmetic and copies ran while one was open for 1% -> 1% of each run, Pallas kernels for 2% -> 4%
where the time goes in v2:
time: 109 us; the launch traced here: 108 us
  blocking collectives  53.4 us (49%)
  starting transfers between devices  26.7 us (24%)
  Pallas kernels  15.3 us (14%)
  local copies, waits for them, and re-layouts  8.7 us (8%)
  waiting for transfers between devices  3.21 us (3%)
    all_to_all x2, blocking collectives, spread(): return lax.all_to_all(y, axis, 0, 0, tiled=True, axis_index_groups=groups)  32.4 us
    all_to_all x1, blocking collectives, scatter_sum(): y = lax.all_to_all(y, axis, 0, 0, tiled=True, axis_index_groups=groups)  21 us
    ppermute x6, starting transfers between devices, shift(): return lax.ppermute(value, 'space', steps)  18.4 us
    ppermute x2, starting transfers between devices, partner(): return lax.ppermute(value, 'space', [(i, i ^ 1) for i in range(n)])  8.27 us
    unnamed x18, local copies, waits for them, and re-layouts  7.86 us
    pallas_call x1, Pallas kernels, local(): call(rest_kernel, [((64, 512), BF16), ((1024, 128), BF16), ((1024, 128),...  6.53 us
    pallas_call x1, Pallas kernels, local(): call(beside_kernel, [((2048, 1024), BF16), ((1024, 256), F32), ((512, 256...  2.61 us
    pallas_call x1, Pallas kernels, local(): call(prepare_kernel, [((1024, 256), F32), ((3072, 256), BF16), ((512, 128...  2.22 us
  transfers between devices with their start and end apart: 8, of which 3 were waited for; matrix products, arithmetic and copies ran while one was open for 1% of the time, Pallas kernels for 4%

profile of v2, /device:TPU:1, one launch (start us, length us, event | category | flops | bytes accessed | tf_op | source)
XLA Modules:
  0.0 108.2 jit_solution(17131142936726977771)
XLA Ops:
  0.6 0.0 copy-start.4
  0.6 1.0 copy-done.4
  1.7 0.0 copy-start.7
  1.7 0.9 copy-done.7
  2.6 0.4 shard_map.84
  3.0 5.4 %collective-permute-start = (bf16[1280,128]{1,0:T(8,128)(2,1)S(1)}, bf16[1280,128]{1,0:T(8,128)(2,1)S(1)}, u32[]{:S(2)}, u32[]{:S(2)}) collective-permute-start(bf16[1280,128]{1,0:T(8,128)(2,1)S(1)} %get-tuple-element.25.last), channel_id=1, source_target_pairs={{0,32},{32,64},{64,96},{96,128},{128,160},{160,192},{192,224},{224... | collective-permute-start | bytes 983048 | tf_op jit(solution)/shard_map/ppermute | solution.py:318
  8.4 4.7 %collective-permute-start.1 = (bf16[1280,128]{1,0:T(8,128)(2,1)S(1)}, bf16[1280,128]{1,0:T(8,128)(2,1)S(1)}, u32[]{:S(2)}, u32[]{:S(2)}) collective-permute-start(bf16[1280,128]{1,0:T(8,128)(2,1)S(1)} %get-tuple-element.26.first), channel_id=1, source_target_pairs={{32,0},{64,32},{96,64},{128,96},{160,128},{192,160},{224,192},{256... | collective-permute-start | bytes 983048 | tf_op jit(solution)/shard_map/ppermute | solution.py:318
  13.1 0.0 copy-start.5
  13.1 1.0 copy-done.5
  14.1 0.0 copy-start.6
  14.1 1.0 copy-done.6
  15.1 0.0 copy-start.8
  15.2 0.9 copy-done.8
  16.1 2.2 %shard_map.85 = (f32[1024,256]{1,0:T(8,128)S(1)}, bf16[3072,256]{1,0:T(8,128)(2,1)S(1)}, bf16[512,128]{1,0:T(8,128)(2,1)S(1)}, bf16[3200,256]{1,0:T(8,128)(2,1)S(1)}, bf16[64,1920]{1,0:T(8,128)(2,1)S(1)}) custom-call(bf16[1280,128]{1,0:T(8,128)(2,1)S(1)} %get-tuple-element.26.first, bf16[1280,128]{1,0:T(8,128)(2,1)S(1)} %get-tuple-element.25.last, ...), custom_call_target="tpu_custom_call" | custom-call | tf_op jit(solution)/shard_map/pallas_call | solution.py:330
  18.3 0.0 collective-permute-done.before
  18.3 0.0 collective-permute-done.1.after
  18.3 2.0 %shard_map.86 = (bf16[512,512]{1,0:T(8,128)(2,1)S(1)}, f32[1024,256]{1,0:T(8,128)S(1)}, bf16[256,128]{1,0:T(8,128)(2,1)}) custom-call(bf16[1280,128]{1,0:T(8,128)(2,1)S(1)} %collective-permute-done.before, bf16[1280,128]{1,0:T(8,128)(2,1)S(1)} %collective-permute-done.1.after, f32[1024,256]{1,0:T(8,128)S(1)} %get-tuple-element.27.part, ...), custom_call_target="tpu_custom_call" | custom-call | tf_op jit(solution)/shard_map/pallas_call | solution.py:335
  20.3 0.0 copy-start
  20.3 1.0 copy-done
  21.2 0.0 copy-start.2
  21.2 0.8 copy-done.2
  22.0 2.5 %collective-permute-start.2 = (bf16[256,128]{1,0:T(8,128)(2,1)}, bf16[256,128]{1,0:T(8,128)(2,1)S(1)}, u32[]{:S(2)}, u32[]{:S(2)}) collective-permute-start(bf16[256,128]{1,0:T(8,128)(2,1)} %get-tuple-element.30.down), channel_id=1, source_target_pairs={{0,64},{32,96},{64,128},{96,160},{128,192},{160,224},{192,256},{22... | collective-permute-start | bytes 196616 | tf_op jit(solution)/shard_map/ppermute | solution.py:318
  24.5 2.6 %collective-permute-start.3 = (bf16[256,128]{1,0:T(8,128)(2,1)}, bf16[256,128]{1,0:T(8,128)(2,1)S(1)}, u32[]{:S(2)}, u32[]{:S(2)}) collective-permute-start(bf16[256,128]{1,0:T(8,128)(2,1)} %get-tuple-element.30.down), channel_id=1, source_target_pairs={{0,32},{32,64},{64,96},{96,128},{128,160},{160,192},{192,224},{224... | collective-permute-start | bytes 196616 | tf_op jit(solution)/shard_map/ppermute | solution.py:318
  27.2 1.9 %collective-permute-start.4 = (bf16[256,128]{1,0:T(8,128)(2,1)}, bf16[256,128]{1,0:T(8,128)(2,1)S(1)}, u32[]{:S(2)}, u32[]{:S(2)}) collective-permute-start(bf16[256,128]{1,0:T(8,128)(2,1)} %get-tuple-element.30.down), channel_id=1, source_target_pairs={{32,0},{64,32},{96,64},{128,96},{160,128},{192,160},{224,192},{256... | collective-permute-start | bytes 196616 | tf_op jit(solution)/shard_map/ppermute | solution.py:318
  29.1 1.3 %collective-permute-start.5 = (bf16[256,128]{1,0:T(8,128)(2,1)}, bf16[256,128]{1,0:T(8,128)(2,1)}, u32[]{:S(2)}, u32[]{:S(2)}) collective-permute-start(bf16[256,128]{1,0:T(8,128)(2,1)} %get-tuple-element.30.down), channel_id=1, source_target_pairs={{64,0},{96,32},{128,64},{160,96},{192,128},{224,160},{256,192},{28... | collective-permute-start | bytes 196616 | tf_op jit(solution)/shard_map/ppermute | solution.py:318
  30.4 0.0 copy-start.1
  30.4 1.2 %copy-done.1 = f32[1024,256]{1,0:T(8,128)S(1)} copy-done((f32[1024,256]{1,0:T(8,128)S(1)}, f32[1024,256]{1,0:T(8,128)}, u32[]{:S(2)}) %copy-start.1) | copy-done | bytes 1048600
  31.6 0.0 copy-start.3
  31.6 2.6 %shard_map.87 = (bf16[2048,1024]{1,0:T(8,128)(2,1)S(1)}, f32[1024,256]{1,0:T(8,128)S(1)}, f32[512,256]{1,0:T(8,128)S(1)}, bf16[512,640]{1,0:T(8,128)(2,1)S(1)}, f32[512,256]{1,0:T(8,128)S(1)}) custom-call(bf16[1280,128]{1,0:T(8,128)(2,1)S(1)} %get-tuple-element.26.first, bf16[1280,128]{1,0:T(8,128)(2,1)S(1)} %get-tuple-element.25.last, ...), custom_call_target="tpu_custom_call" | custom-call | tf_op jit(solution)/shard_map/pallas_call | solution.py:341
  34.3 0.0 collective-permute-done.2.d0
  34.3 0.0 collective-permute-done.3.d1
  34.3 0.0 collective-permute-done.4.d3
  34.3 1.7 %collective-permute-done.5.d4 = bf16[256,128]{1,0:T(8,128)(2,1)} collective-permute-done((bf16[256,128]{1,0:T(8,128)(2,1)}, bf16[256,128]{1,0:T(8,128)(2,1)}, u32[]{:S(2)}, u32[]{:S(2)}) %collective-permute-start.5) | collective-permute-done | bytes 65568 | tf_op jit(solution)/shard_map/ppermute | solution.py:318
  36.0 0.0 copy-done.3
  36.0 6.5 %shard_map.88 = (bf16[64,512]{1,0:T(8,128)(2,1)S(1)}, bf16[1024,128]{1,0:T(8,128)(2,1)S(1)}, bf16[1024,128]{1,0:T(8,128)(2,1)S(1)}) custom-call(s32[1]{0:T(128)} %bitcast.core, bf16[256,128]{1,0:T(8,128)(2,1)S(1)} %collective-permute-done.2.d0, bf16[256,128]{1,0:T(8,128)(2,1)S(1)} %collective-permute-done.3.d1, ...), custom_call_target="tpu_custom_call" | custom-call | tf_op jit(solution)/shard_map/pallas_call | solution.py:346
  42.5 2.3 %collective-permute-start.6 = (bf16[1024,128]{1,0:T(8,128)(2,1)S(1)}, bf16[1024,128]{1,0:T(8,128)(2,1)S(1)}, u32[]{:S(2)}, u32[]{:S(2)}) collective-permute-start(bf16[1024,128]{1,0:T(8,128)(2,1)S(1)} %get-tuple-element.42), channel_id=1, source_target_pairs={{0,32},{32,0},{64,96},{96,64},{128,160},{160,128},{192,224},{224,1... | collective-permute-start | bytes 786440 | tf_op jit(solution)/shard_map/ppermute | solution.py:321
  44.8 1.1 %collective-permute-done.6 = bf16[1024,128]{1,0:T(8,128)(2,1)S(1)} collective-permute-done((bf16[1024,128]{1,0:T(8,128)(2,1)S(1)}, bf16[1024,128]{1,0:T(8,128)(2,1)S(1)}, u32[]{:S(2)}, u32[]{:S(2)}) %collective-permute-start.6) | collective-permute-done | bytes 262176 | tf_op jit(solution)/shard_map/ppermute | solution.py:321
  46.0 0.1 add_convert_fusion
  46.1 21.0 %all_to_all.15 = bf16[32,32,128]{2,1,0:T(8,128)(2,1)S(1)} all-to-all(bf16[32,32,128]{2,1,0:T(8,128)(2,1)S(1)} %bitcast.16), channel_id=1, replica_groups=mesh['space'=16,'dp'=32] {'dp'}, dimensions={0} | all-to-all | bytes 524288 | tf_op jit(solution)/shard_map/all_to_all | solution.py:304
  67.1 0.1 reduce_sum.24
  67.2 17.4 %all_to_all.16 = bf16[8,32,128]{2,1,0:T(8,128)(2,1)S(1)} all-to-all(bf16[8,32,128]{2,1,0:T(8,128)(2,1)S(1)} %broadcast_in_dim.4), channel_id=1, replica_groups={{0,64,128,192,256,320,384,448},{32,96,160,224,288,352,416,480},{1,65,12..., dimensions={0} | all-to-all | bytes 131072 | tf_op jit(solution)/shard_map/all_to_all | solution.py:310
  84.6 15.0 %all_to_all.17 = bf16[32,32,128]{2,1,0:T(8,128)(2,1)S(1)} all-to-all(bf16[32,32,128]{2,1,0:T(8,128)(2,1)S(1)} %broadcast_in_dim.5), channel_id=1, replica_groups=mesh['space'=16,'dp'=32] {'dp'}, dimensions={0} | all-to-all | bytes 524288 | tf_op jit(solution)/shard_map/all_to_all | solution.py:310
  99.6 6.0 %collective-permute-start.7 = (bf16[1024,128]{1,0:T(8,128)(2,1)S(1)}, bf16[1024,128]{1,0:T(8,128)(2,1)S(1)}, u32[]{:S(2)}, u32[]{:S(2)}) collective-permute-start(bf16[1024,128]{1,0:T(8,128)(2,1)S(1)} %bitcast.9), channel_id=1, source_target_pairs={{0,32},{32,0},{64,96},{96,64},{128,160},{160,128},{192,224},{224,1... | collective-permute-start | bytes 786440 | tf_op jit(solution)/shard_map/ppermute | solution.py:321
  105.6 0.8 reshape.43
  106.4 0.4 collective-permute-done.7.other
  106.7 1.5 %shard_map.89 = (f32[3,3,3,64,64]{4,3,2,1,0:T(8,128)}, f32[2,2,2,64,64]{4,3,2,1,0:T(8,128)}, f32[3,3,3,64,64]{4,3,2,1,0:T(8,128)}) custom-call(s32[1]{0:T(128)} %bitcast.core, bf16[1024,128]{1,0:T(8,128)(2,1)S(1)} %bitcast.10, bf16[1024,128]{1,0:T(8,128)(2,1)S(1)} %collective-permute-done.7.other), custom_call_target="tpu_custom_call" | custom-call | tf_op jit(solution)/shard_map/pallas_call | solution.py:357
  (3 shorter events, 0.1 us)
Async XLA Ops:
  0.6 1.0 copy-start.4
  1.7 0.9 copy-start.7
  3.0 15.3 %collective-permute-start = (bf16[1280,128]{1,0:T(8,128)(2,1)S(1)}, bf16[1280,128]{1,0:T(8,128)(2,1)S(1)}, u32[]{:S(2)}, u32[]{:S(2)}) collective-permute-start(bf16[1280,128]{1,0:T(8,128)(2,1)S(1)} %get-tuple-element.25.last), channel_id=1, source_target_pairs={{0,32},{32,64},{64,96},{96,128},{128,160},{160,192},{192,224},{224... | collective-permute-start | bytes 983048 | tf_op jit(solution)/shard_map/ppermute | solution.py:318
  8.4 9.9 %collective-permute-start.1 = (bf16[1280,128]{1,0:T(8,128)(2,1)S(1)}, bf16[1280,128]{1,0:T(8,128)(2,1)S(1)}, u32[]{:S(2)}, u32[]{:S(2)}) collective-permute-start(bf16[1280,128]{1,0:T(8,128)(2,1)S(1)} %get-tuple-element.26.first), channel_id=1, source_target_pairs={{32,0},{64,32},{96,64},{128,96},{160,128},{192,160},{224,192},{256... | collective-permute-start | bytes 983048 | tf_op jit(solution)/shard_map/ppermute | solution.py:318
  13.1 1.0 copy-start.5
  14.1 1.0 copy-start.6
  15.1 0.9 copy-start.8
  20.3 1.0 copy-start
  21.2 0.8 copy-start.2
  22.0 12.2 %collective-permute-start.2 = (bf16[256,128]{1,0:T(8,128)(2,1)}, bf16[256,128]{1,0:T(8,128)(2,1)S(1)}, u32[]{:S(2)}, u32[]{:S(2)}) collective-permute-start(bf16[256,128]{1,0:T(8,128)(2,1)} %get-tuple-element.30.down), channel_id=1, source_target_pairs={{0,64},{32,96},{64,128},{96,160},{128,192},{160,224},{192,256},{22... | collective-permute-start | bytes 196616 | tf_op jit(solution)/shard_map/ppermute | solution.py:318
  24.5 9.7 %collective-permute-start.3 = (bf16[256,128]{1,0:T(8,128)(2,1)}, bf16[256,128]{1,0:T(8,128)(2,1)S(1)}, u32[]{:S(2)}, u32[]{:S(2)}) collective-permute-start(bf16[256,128]{1,0:T(8,128)(2,1)} %get-tuple-element.30.down), channel_id=1, source_target_pairs={{0,32},{32,64},{64,96},{96,128},{128,160},{160,192},{192,224},{224... | collective-permute-start | bytes 196616 | tf_op jit(solution)/shard_map/ppermute | solution.py:318
  27.2 7.1 %collective-permute-start.4 = (bf16[256,128]{1,0:T(8,128)(2,1)}, bf16[256,128]{1,0:T(8,128)(2,1)S(1)}, u32[]{:S(2)}, u32[]{:S(2)}) collective-permute-start(bf16[256,128]{1,0:T(8,128)(2,1)} %get-tuple-element.30.down), channel_id=1, source_target_pairs={{32,0},{64,32},{96,64},{128,96},{160,128},{192,160},{224,192},{256... | collective-permute-start | bytes 196616 | tf_op jit(solution)/shard_map/ppermute | solution.py:318
  29.1 6.9 %collective-permute-start.5 = (bf16[256,128]{1,0:T(8,128)(2,1)}, bf16[256,128]{1,0:T(8,128)(2,1)}, u32[]{:S(2)}, u32[]{:S(2)}) collective-permute-start(bf16[256,128]{1,0:T(8,128)(2,1)} %get-tuple-element.30.down), channel_id=1, source_target_pairs={{64,0},{96,32},{128,64},{160,96},{192,128},{224,160},{256,192},{28... | collective-permute-start | bytes 196616 | tf_op jit(solution)/shard_map/ppermute | solution.py:318
  30.4 1.2 %copy-start.1 = (f32[1024,256]{1,0:T(8,128)S(1)}, f32[1024,256]{1,0:T(8,128)}, u32[]{:S(2)}) copy-start(f32[1024,256]{1,0:T(8,128)} %copy-done) | copy-start | bytes 3145732
  31.6 4.4 %copy-start.3 = (bf16[512,512]{1,0:T(8,128)(2,1)S(1)}, bf16[512,512]{1,0:T(8,128)(2,1)}, u32[]{:S(2)}) copy-start(bf16[512,512]{1,0:T(8,128)(2,1)} %copy-done.2) | copy-start | bytes 1572868
  42.5 3.5 %collective-permute-start.6 = (bf16[1024,128]{1,0:T(8,128)(2,1)S(1)}, bf16[1024,128]{1,0:T(8,128)(2,1)S(1)}, u32[]{:S(2)}, u32[]{:S(2)}) collective-permute-start(bf16[1024,128]{1,0:T(8,128)(2,1)S(1)} %get-tuple-element.42), channel_id=1, source_target_pairs={{0,32},{32,0},{64,96},{96,64},{128,160},{160,128},{192,224},{224,1... | collective-permute-start | bytes 786440 | tf_op jit(solution)/shard_map/ppermute | solution.py:321
  99.6 7.1 %collective-permute-start.7 = (bf16[1024,128]{1,0:T(8,128)(2,1)S(1)}, bf16[1024,128]{1,0:T(8,128)(2,1)S(1)}, u32[]{:S(2)}, u32[]{:S(2)}) collective-permute-start(bf16[1024,128]{1,0:T(8,128)(2,1)S(1)} %bitcast.9), channel_id=1, source_target_pairs={{0,32},{32,0},{64,96},{96,64},{128,160},{160,128},{192,224},{224,1... | collective-permute-start | bytes 786440 | tf_op jit(solution)/shard_map/ppermute | solution.py:321

commit v3 on v2

--- a/solution.py
+++ b/solution.py
@@ -75,12 +75,18 @@
     return jnp.concatenate([jnp.where(low, field, swapped), jnp.where(low, swapped, field)], 0)
 
 
-def edges_kernel(volumes, cot, first, last, planes, rows):
+def edges_kernel(volumes, cot, first, last, raw, raw_cot, planes, rows, sems):
+    copies = [pltpu.make_async_copy(volumes.at[:, x], raw.at[x], sems.at[x]) for x in range(2)]
+    copies.append(pltpu.make_async_copy(cot, raw_cot, sems.at[2]))
+    for copy in copies:
+        copy.start()
     for x, out in enumerate((first, last)):
-        planes[x] = volumes[:, x].astype(F32).reshape(1024, 128)
+        copies[x].wait()
+        planes[x] = raw[x].astype(F32).reshape(1024, 128)
         for y in range(16):
             out[y * 64 : y * 64 + 64] = planes[x, pl.ds(y, 64, stride=16), :].astype(BF16)
-    rows[...] = cot[...].astype(F32).reshape(512, 64)
+    copies[2].wait()
+    rows[...] = raw_cot[...].astype(F32).reshape(512, 64)
     for j in range(4):
         both = jnp.concatenate(
             [rows[pl.ds(j, 64, stride=8), :], rows[pl.ds(j + 4, 64, stride=8), :]], 0
@@ -90,7 +96,13 @@
             out[1024 + j * 64 : 1088 + j * 64] = block
 
 
-def prepare_kernel(first, last, w_first, w_down, w_coarse, part, fw, dw, cw, bw, taps):
+def prepare_kernel(
+    first, last, far_first, far_down, part, fw, dw, taps, w_first, w_down, sems
+):
+    weights = ((far_first, w_first), (far_down, w_down))
+    copies = [pltpu.make_async_copy(far, to, sems.at[i]) for i, (far, to) in enumerate(weights)]
+    for copy in copies:
+        copy.start()
     low = low_lanes((64, 128))
     zero = jnp.zeros((64, 128), BF16)
     pair = twice()
@@ -98,6 +110,10 @@
     def both(ref, k):
         return dot(ref[k * 64 : k * 64 + 64], pair).astype(BF16)
 
+    for x, ref in enumerate((first, last)):
+        gather_taps(ref[0:1024], taps.at[:, x * 1024 : x * 1024 + 1024])
+    for copy in copies:
+        copy.wait()
     for dx in range(3):
         for tz in range(4):
             for qz in range(2):
@@ -122,6 +138,46 @@
                 k = x * 4 + qy * 2 + qz
                 at = (x * 4 + qz * 2 + qy) * 64
                 dw[at : at + 64] = both(w_down, k)
+    for x in range(2):
+        part[x * 512 : x * 512 + 512] = dot(taps[...], fw[1024 - x * 1024 : 3072 - x * 1024])
+
+
+def first_kernel(before, after, part, fw, dw, act, pre, send, taps):
+    low = low_lanes((256, 128))
+    for x, side in enumerate((before, after)):
+        gather_taps(side[0:1024], taps)
+        value = part[x * 512 : x * 512 + 512] + dot(taps[...], fw[x * 2048 : x * 2048 + 1024])
+        pre[x * 512 : x * 512 + 512] = value
+        act[:, x * 256 : x * 256 + 256] = (value * jax.nn.sigmoid(value)).astype(BF16)
+    down = dot(act[...], dw[...])
+    send[...] = jnp.where(low, down[:256], down[256:]).astype(BF16)
+
+
+def beside_kernel(
+    first, before, after, pre, down, far_coarse, cw, bw, slope, ct, own, acc, w_coarse, sem
+):
+    copy = pltpu.make_async_copy(far_coarse, w_coarse, sem)
+    copy.start()
+    value = pre[...]
+    s = jax.nn.sigmoid(value)
+    slope[...] = s * (1.0 + value * (1.0 - s))
+    low = low_lanes((256, 128))
+    f0, t0 = turned(before[1024:1280])
+    f1, t1 = turned(first[1024:1280])
+    f2, t2 = turned(after[1024:1280])
+    ct[0:256, 0:128] = jnp.where(low, f0, t1)
+    ct[256:512, 0:128] = jnp.where(low, t0, f1)
+    ct[0:256, 128:256] = f2
+    ct[256:512, 128:256] = t2
+    gather_coarse(doubled(down[...]), own)
+    low = low_lanes((64, 128))
+    zero = jnp.zeros((64, 128), BF16)
+    pair = twice()
+
+    def both(ref, k):
+        return dot(ref[k * 64 : k * 64 + 64], pair).astype(BF16)
+
+    copy.wait()
     order = [(0, 0), (0, 2), (1, 0), (1, 2), (2, 0), (2, 2), (0, 1), (2, 1), (1, 1), None]
     for j, tap in enumerate(order):
         if tap is None:
@@ -141,45 +197,16 @@
         for j in range(5):
             at = dx * 640 + j * 128
             bw[:, at : at + 128] = jnp.where(low, back[2 * j], back[2 * j + 1])
-    for x, ref in enumerate((first, last)):
-        gather_taps(ref[0:1024], taps.at[:, x * 1024 : x * 1024 + 1024])
-    for x in range(2):
-        part[x * 512 : x * 512 + 512] = dot(taps[...], fw[1024 - x * 1024 : 3072 - x * 1024])
-
-
-def first_kernel(before, after, part, fw, dw, act, pre, send, taps):
-    low = low_lanes((256, 128))
-    for x, side in enumerate((before, after)):
-        gather_taps(side[0:1024], taps)
-        value = part[x * 512 : x * 512 + 512] + dot(taps[...], fw[x * 2048 : x * 2048 + 1024])
-        pre[x * 512 : x * 512 + 512] = value
-        act[:, x * 256 : x * 256 + 256] = (value * jax.nn.sigmoid(value)).astype(BF16)
-    down = dot(act[...], dw[...])
-    send[...] = jnp.where(low, down[:256], down[256:]).astype(BF16)
-
-
-def beside_kernel(first, last, before, after, pre, down, cw, taps, slope, ct, own, acc):
-    value = pre[...]
-    s = jax.nn.sigmoid(value)
-    slope[...] = s * (1.0 + value * (1.0 - s))
+    acc[...] = dot(own[...], cw[1280:1920])
+
+
+def rest_kernel(
+    core, d0, d1, d3, d4, first, last, before, after, act, slope, ct, own, acc, dw, cw, bw, out, keep, send,
+    grads, below, above, near, taps,
+):
+    low = low_lanes((64, 128))
     for p, ref in enumerate((before, first, last, after)):
         gather_taps(ref[0:1024], taps.at[p * 512 : p * 512 + 512])
-    low = low_lanes((256, 128))
-    f0, t0 = turned(before[1024:1280])
-    f1, t1 = turned(first[1024:1280])
-    f2, t2 = turned(after[1024:1280])
-    ct[0:256, 0:128] = jnp.where(low, f0, t1)
-    ct[256:512, 0:128] = jnp.where(low, t0, f1)
-    ct[0:256, 128:256] = f2
-    ct[256:512, 128:256] = t2
-    gather_coarse(doubled(down[...]), own)
-    acc[...] = dot(own[...], cw[1280:1920])
-
-
-def rest_kernel(
-    core, d0, d1, d3, d4, act, slope, taps, ct, own, acc, dw, cw, bw, out, keep, send, grads, below, above, near
-):
-    low = low_lanes((64, 128))
     for p, ref in enumerate((d0, d1)):
         gather_coarse(doubled(ref[...]), below.at[:, p * 640 : p * 640 + 640])
     for p, ref in enumerate((d3, d4)):
@@ -284,19 +311,20 @@
             down[j // 2, qy, j % 2] = t[qy * 64 : qy * 64 + 64]
 
 
-def call(kernel, outs, scratch=(), scalars=0):
-    specs = {}
-    if scalars:
-        specs["in_specs"] = [pl.BlockSpec(memory_space=pltpu.SMEM)] + [
-            pl.BlockSpec(memory_space=pltpu.VMEM)
-        ] * (scalars - 1)
+def call(kernel, outs, scratch=(), places=""):
+    kinds = {"s": pltpu.SMEM, "h": pltpu.HBM, "v": pltpu.VMEM}
+    specs = {"in_specs": [pl.BlockSpec(memory_space=kinds[p]) for p in places]} if places else {}
     return pl.pallas_call(
         kernel,
         out_shape=[jax.ShapeDtypeStruct(s, d) for s, d in outs],
-        scratch_shapes=[pltpu.VMEM(s, d) for s, d in scratch],
+        scratch_shapes=[pltpu.VMEM(*s) if isinstance(s, tuple) else s for s in scratch],
         compiler_params=PARAMS,
         **specs,
     )
+
+
+def far(value):
+    return pltpu.with_memory_space_constraint(value, pltpu.HBM)
 
 
 def scatter_sum(y, axis, count, groups=None):
@@ -323,32 +351,55 @@
     first, last = call(
         edges_kernel,
         [((1280, 128), BF16)] * 2,
-        [((2, 1024, 128), F32), ((512, 64), F32)],
-    )(volumes.reshape(64, 2, 16, 128), cotangent.reshape(64, 8, 64))
+        [
+            ((2, 64, 16, 128), BF16),
+            ((64, 8, 64), BF16),
+            ((2, 1024, 128), F32),
+            ((512, 64), F32),
+            pltpu.SemaphoreType.DMA((3,)),
+        ],
+        "hh",
+    )(far(volumes.reshape(64, 2, 16, 128)), far(cotangent.reshape(64, 8, 64)))
     before = shift(last, 1)
     after = shift(first, -1)
-    part, fw, dw, cw, bw = call(
+    part, fw, dw = call(
         prepare_kernel,
-        [((1024, 256), F32), ((3072, 256), BF16), ((512, 128), BF16), ((3200, 256), BF16), ((64, 1920), BF16)],
-        [((512, 2048), BF16)],
-    )(first, last, w_first.reshape(1728, 64), w_down.reshape(512, 64), w_coarse.reshape(1728, 64))
+        [((1024, 256), F32), ((3072, 256), BF16), ((512, 128), BF16)],
+        [((512, 2048), BF16), ((1728, 64), BF16), ((512, 64), BF16), pltpu.SemaphoreType.DMA((2,))],
+        "vvhh",
+    )(first, last, far(w_first.reshape(1728, 64)), far(w_down.reshape(512, 64)))
     act, pre, down = call(
         first_kernel,
         [((512, 512), BF16), ((1024, 256), F32), ((256, 128), BF16)],
         [((512, 1024), BF16)],
     )(before, after, part, fw, dw)
     halo = [shift(down, 2), shift(down, 1), shift(down, -1), shift(down, -2)]
-    taps, slope, ct, own, acc = call(
+    cw, bw, slope, ct, own, acc = call(
         beside_kernel,
-        [((2048, 1024), BF16), ((1024, 256), F32), ((512, 256), F32), ((512, 640), BF16), ((512, 256), F32)],
-    )(first, last, before, after, pre, down, cw)
+        [
+            ((3200, 256), BF16),
+            ((64, 1920), BF16),
+            ((1024, 256), F32),
+            ((512, 256), F32),
+            ((512, 640), BF16),
+            ((512, 256), F32),
+        ],
+        [((1728, 64), BF16), pltpu.SemaphoreType.DMA],
+        "vvvvvh",
+    )(first, before, after, pre, down, far(w_coarse.reshape(1728, 64)))
     core = lax.rem(lax.axis_index("space"), 2).reshape(1)
     out, keep, send = call(
         rest_kernel,
         [((64, 512), BF16), ((1024, 128), BF16), ((1024, 128), BF16)],
-        [((2048, 128), BF16), ((512, 1280), BF16), ((512, 1280), BF16), ((512, 1920), BF16)],
-        scalars=14,
-    )(core, *halo, act, slope, taps, ct, own, acc, dw, cw, bw)
+        [
+            ((2048, 128), BF16),
+            ((512, 1280), BF16),
+            ((512, 1280), BF16),
+            ((512, 1920), BF16),
+            ((2048, 1024), BF16),
+        ],
+        "s" + 16 * "v",
+    )(core, *halo, first, last, before, after, act, slope, ct, own, acc, dw, cw, bw)
     half = (keep.astype(F32) + partner(send).astype(F32)).astype(BF16)
     chips = [list(range(c, n, 2)) for c in range(2)]
     piece = scatter_sum(half, "dp", m)
@@ -358,7 +409,7 @@
         unpack_kernel,
         [((3, 3, 3, 64, 64), F32), ((2, 2, 2, 64, 64), F32), ((3, 3, 3, 64, 64), F32)],
         [((2048, 128), BF16)],
-        scalars=3,
+        "svv",
     )(core, mine, partner(mine))
     return (out.reshape(1, 64, 1, 8, 64), grad_first, grad_down, grad_coarse)
 

time: 109 us -> 104 us (0.954)
  local copies, waits for them, and re-layouts: 8.7 us -> 0.84 us
  starting transfers between devices: 26.7 us -> 29 us
  waiting for transfers between devices: 3.21 us -> 4.99 us
  blocking collectives: 53.4 us -> 52.1 us
    unnamed x18 -> x0, local copies, waits for them, and re-layouts: 7.86 us -> none
    ppermute x6, starting transfers between devices: 18.4 us -> 20.2 us  [shift(): return lax.ppermute(value, 'space', steps)]
    ppermute x6, waiting for transfers between devices: 1.72 us -> 3.5 us  [shift(): return lax.ppermute(value, 'space', steps)]
  transfers between devices with their start and end apart: 8 -> 8, of which waited for: 3 -> 5; matrix products, arithmetic and copies ran while one was open for 1% -> 1% of each run, Pallas kernels for 4% -> 4%
where the time goes in v3:
time: 104 us; the launch traced here: 103 us
  blocking collectives  52.1 us (50%)
  starting transfers between devices  29 us (28%)
  Pallas kernels  15.6 us (15%)
  waiting for transfers between devices  4.99 us (5%)
    all_to_all x2, blocking collectives, spread(): return lax.all_to_all(y, axis, 0, 0, tiled=True, axis_index_groups=groups)  31.6 us
    all_to_all x1, blocking collectives, scatter_sum(): y = lax.all_to_all(y, axis, 0, 0, tiled=True, axis_index_groups=groups)  20.5 us
    ppermute x6, starting transfers between devices, shift(): return lax.ppermute(value, 'space', steps)  20.2 us
    ppermute x2, starting transfers between devices, partner(): return lax.ppermute(value, 'space', [(i, i ^ 1) for i in range(n)])  8.77 us
    pallas_call x1, Pallas kernels, local(): call(rest_kernel, [((64, 512), BF16), ((1024, 128), BF16), ((1024, 128),...  6.66 us
    ppermute x6, waiting for transfers between devices, shift(): return lax.ppermute(value, 'space', steps)  3.5 us
    pallas_call x1, Pallas kernels, local(): call(prepare_kernel, [((1024, 256), F32), ((3072, 256), BF16), ((512, 128...  2.89 us
  transfers between devices with their start and end apart: 8, of which 5 were waited for; matrix products, arithmetic and copies ran while one was open for 1% of the time, Pallas kernels for 4%

profile of v3, /device:TPU:1, one launch (start us, length us, event | category | flops | bytes accessed | tf_op | source)
XLA Modules:
  0.0 103.5 jit_solution(14452500075966159118)
XLA Ops:
  0.6 1.5 %shard_map.84 = (bf16[1280,128]{1,0:T(8,128)(2,1)S(1)}, bf16[1280,128]{1,0:T(8,128)(2,1)S(1)}) custom-call(bf16[64,2,16,128]{3,2,1,0:T(8,128)(2,1)} %bitcast.12, bf16[64,8,64]{2,1,0:T(8,128)(2,1)} %bitcast.15), custom_call_target="tpu_custom_call" | custom-call | tf_op jit(solution)/shard_map/pallas_call | solution.py:351
  2.1 8.8 %collective-permute-start.1 = (bf16[1280,128]{1,0:T(8,128)(2,1)S(1)}, bf16[1280,128]{1,0:T(8,128)(2,1)S(1)}, u32[]{:S(2)}, u32[]{:S(2)}) collective-permute-start(bf16[1280,128]{1,0:T(8,128)(2,1)S(1)} %get-tuple-element.25.first), channel_id=1, source_target_pairs={{32,0},{64,32},{96,64},{128,96},{160,128},{192,160},{224,192},{256... | collective-permute-start | bytes 983048 | tf_op jit(solution)/shard_map/ppermute | solution.py:346
  10.9 1.9 %collective-permute-start = (bf16[1280,128]{1,0:T(8,128)(2,1)S(1)}, bf16[1280,128]{1,0:T(8,128)(2,1)S(1)}, u32[]{:S(2)}, u32[]{:S(2)}) collective-permute-start(bf16[1280,128]{1,0:T(8,128)(2,1)S(1)} %get-tuple-element.24.last), channel_id=1, source_target_pairs={{0,32},{32,64},{64,96},{96,128},{128,160},{160,192},{192,224},{224... | collective-permute-start | bytes 983048 | tf_op jit(solution)/shard_map/ppermute | solution.py:346
  12.8 2.9 %shard_map.85 = (f32[1024,256]{1,0:T(8,128)S(1)}, bf16[3072,256]{1,0:T(8,128)(2,1)S(1)}, bf16[512,128]{1,0:T(8,128)(2,1)S(1)}) custom-call(bf16[1280,128]{1,0:T(8,128)(2,1)S(1)} %get-tuple-element.25.first, bf16[1280,128]{1,0:T(8,128)(2,1)S(1)} %get-tuple-element.24.last, bf16[1728,64]{1,0:T(8,128)(2,1)} %bitcast.13, bf16[512,64]{1,0:T(8,128)(2,1)} %bitcast.16), custom_call_target="tpu_custom_call" | custom-call | tf_op jit(solution)/shard_map/pallas_call | solution.py:365
  15.7 0.0 collective-permute-done.1.after
  15.7 1.1 %collective-permute-done.before = bf16[1280,128]{1,0:T(8,128)(2,1)S(1)} collective-permute-done((bf16[1280,128]{1,0:T(8,128)(2,1)S(1)}, bf16[1280,128]{1,0:T(8,128)(2,1)S(1)}, u32[]{:S(2)}, u32[]{:S(2)}) %collective-permute-start) | collective-permute-done | bytes 327712 | tf_op jit(solution)/shard_map/ppermute | solution.py:346
  16.8 1.3 %shard_map.86 = (bf16[512,512]{1,0:T(8,128)(2,1)S(1)}, f32[1024,256]{1,0:T(8,128)S(1)}, bf16[256,128]{1,0:T(8,128)(2,1)S(1)}) custom-call(bf16[1280,128]{1,0:T(8,128)(2,1)S(1)} %collective-permute-done.before, bf16[1280,128]{1,0:T(8,128)(2,1)S(1)} %collective-permute-done.1.after, f32[1024,256]{1,0:T(8,128)S(1)} %get-tuple-element.26.part, ...), custom_call_target="tpu_custom_call" | custom-call | tf_op jit(solution)/shard_map/pallas_call | solution.py:371
  18.2 1.3 %collective-permute-start.2 = (bf16[256,128]{1,0:T(8,128)(2,1)S(1)}, bf16[256,128]{1,0:T(8,128)(2,1)S(1)}, u32[]{:S(2)}, u32[]{:S(2)}) collective-permute-start(bf16[256,128]{1,0:T(8,128)(2,1)S(1)} %get-tuple-element.29.down), channel_id=1, source_target_pairs={{0,64},{32,96},{64,128},{96,160},{128,192},{160,224},{192,256},{22... | collective-permute-start | bytes 196616 | tf_op jit(solution)/shard_map/ppermute | solution.py:346
  19.5 5.0 %collective-permute-start.3 = (bf16[256,128]{1,0:T(8,128)(2,1)S(1)}, bf16[256,128]{1,0:T(8,128)(2,1)S(1)}, u32[]{:S(2)}, u32[]{:S(2)}) collective-permute-start(bf16[256,128]{1,0:T(8,128)(2,1)S(1)} %get-tuple-element.29.down), channel_id=1, source_target_pairs={{0,32},{32,64},{64,96},{96,128},{128,160},{160,192},{192,224},{224... | collective-permute-start | bytes 196616 | tf_op jit(solution)/shard_map/ppermute | solution.py:346
  24.5 1.9 %collective-permute-start.4 = (bf16[256,128]{1,0:T(8,128)(2,1)S(1)}, bf16[256,128]{1,0:T(8,128)(2,1)S(1)}, u32[]{:S(2)}, u32[]{:S(2)}) collective-permute-start(bf16[256,128]{1,0:T(8,128)(2,1)S(1)} %get-tuple-element.29.down), channel_id=1, source_target_pairs={{32,0},{64,32},{96,64},{128,96},{160,128},{192,160},{224,192},{256... | collective-permute-start | bytes 196616 | tf_op jit(solution)/shard_map/ppermute | solution.py:346
  26.4 1.3 %collective-permute-start.5 = (bf16[256,128]{1,0:T(8,128)(2,1)S(1)}, bf16[256,128]{1,0:T(8,128)(2,1)S(1)}, u32[]{:S(2)}, u32[]{:S(2)}) collective-permute-start(bf16[256,128]{1,0:T(8,128)(2,1)S(1)} %get-tuple-element.29.down), channel_id=1, source_target_pairs={{64,0},{96,32},{128,64},{160,96},{192,128},{224,160},{256,192},{28... | collective-permute-start | bytes 196616 | tf_op jit(solution)/shard_map/ppermute | solution.py:346
  27.7 1.8 %shard_map.87 = (bf16[3200,256]{1,0:T(8,128)(2,1)S(1)}, bf16[64,1920]{1,0:T(8,128)(2,1)S(1)}, f32[1024,256]{1,0:T(8,128)S(1)}, f32[512,256]{1,0:T(8,128)S(1)}, b...) custom-call(bf16[1280,128]{1,0:T(8,128)(2,1)S(1)} %get-tuple-element.25.first, ...), custom_call_target="tpu_custom_call" | custom-call | tf_op jit(solution)/shard_map/pallas_call | solution.py:377
  29.5 0.0 collective-permute-done.2.d0
  29.5 0.0 collective-permute-done.3.d1
  29.5 0.6 collective-permute-done.4.d3
  30.1 1.8 %collective-permute-done.5.d4 = bf16[256,128]{1,0:T(8,128)(2,1)S(1)} collective-permute-done((bf16[256,128]{1,0:T(8,128)(2,1)S(1)}, bf16[256,128]{1,0:T(8,128)(2,1)S(1)}, u32[]{:S(2)}, u32[]{:S(2)}) %collective-permute-start.5) | collective-permute-done | bytes 65568 | tf_op jit(solution)/shard_map/ppermute | solution.py:346
  31.9 6.7 %shard_map.88 = (bf16[64,512]{1,0:T(8,128)(2,1)S(1)}, bf16[1024,128]{1,0:T(8,128)(2,1)S(1)}, bf16[1024,128]{1,0:T(8,128)(2,1)S(1)}) custom-call(s32[1]{0:T(128)} %bitcast.core, bf16[256,128]{1,0:T(8,128)(2,1)S(1)} %collective-permute-done.2.d0, bf16[256,128]{1,0:T(8,128)(2,1)S(1)} %collective-permute-done.3.d1, ...), custom_call_target="tpu_custom_call" | custom-call | tf_op jit(solution)/shard_map/pallas_call | solution.py:391
  38.6 2.8 %collective-permute-start.6 = (bf16[1024,128]{1,0:T(8,128)(2,1)S(1)}, bf16[1024,128]{1,0:T(8,128)(2,1)S(1)}, u32[]{:S(2)}, u32[]{:S(2)}) collective-permute-start(bf16[1024,128]{1,0:T(8,128)(2,1)S(1)} %get-tuple-element.40), channel_id=1, source_target_pairs={{0,32},{32,0},{64,96},{96,64},{128,160},{160,128},{192,224},{224,1... | collective-permute-start | bytes 786440 | tf_op jit(solution)/shard_map/ppermute | solution.py:349
  41.4 1.1 %collective-permute-done.6 = bf16[1024,128]{1,0:T(8,128)(2,1)S(1)} collective-permute-done((bf16[1024,128]{1,0:T(8,128)(2,1)S(1)}, bf16[1024,128]{1,0:T(8,128)(2,1)S(1)}, u32[]{:S(2)}, u32[]{:S(2)}) %collective-permute-start.6) | collective-permute-done | bytes 262176 | tf_op jit(solution)/shard_map/ppermute | solution.py:349
  42.5 0.1 add_convert_fusion
  42.6 20.5 %all_to_all.15 = bf16[32,32,128]{2,1,0:T(8,128)(2,1)S(1)} all-to-all(bf16[32,32,128]{2,1,0:T(8,128)(2,1)S(1)} %bitcast.11), channel_id=1, replica_groups=mesh['space'=16,'dp'=32] {'dp'}, dimensions={0} | all-to-all | bytes 524288 | tf_op jit(solution)/shard_map/all_to_all | solution.py:332
  63.1 0.1 reduce_sum.24
  63.2 16.6 %all_to_all.16 = bf16[8,32,128]{2,1,0:T(8,128)(2,1)S(1)} all-to-all(bf16[8,32,128]{2,1,0:T(8,128)(2,1)S(1)} %broadcast_in_dim.4), channel_id=1, replica_groups={{0,64,128,192,256,320,384,448},{32,96,160,224,288,352,416,480},{1,65,12..., dimensions={0} | all-to-all | bytes 131072 | tf_op jit(solution)/shard_map/all_to_all | solution.py:338
  79.9 15.0 %all_to_all.17 = bf16[32,32,128]{2,1,0:T(8,128)(2,1)S(1)} all-to-all(bf16[32,32,128]{2,1,0:T(8,128)(2,1)S(1)} %broadcast_in_dim.5), channel_id=1, replica_groups=mesh['space'=16,'dp'=32] {'dp'}, dimensions={0} | all-to-all | bytes 524288 | tf_op jit(solution)/shard_map/all_to_all | solution.py:338
  94.8 6.0 %collective-permute-start.7 = (bf16[1024,128]{1,0:T(8,128)(2,1)S(1)}, bf16[1024,128]{1,0:T(8,128)(2,1)S(1)}, u32[]{:S(2)}, u32[]{:S(2)}) collective-permute-start(bf16[1024,128]{1,0:T(8,128)(2,1)S(1)} %bitcast.9), channel_id=1, source_target_pairs={{0,32},{32,0},{64,96},{96,64},{128,160},{160,128},{192,224},{224,1... | collective-permute-start | bytes 786440 | tf_op jit(solution)/shard_map/ppermute | solution.py:349
  100.8 0.8 reshape.43
  101.6 0.4 collective-permute-done.7.other
  101.9 1.5 %shard_map.89 = (f32[3,3,3,64,64]{4,3,2,1,0:T(8,128)}, f32[2,2,2,64,64]{4,3,2,1,0:T(8,128)}, f32[3,3,3,64,64]{4,3,2,1,0:T(8,128)}) custom-call(s32[1]{0:T(128)} %bitcast.core, bf16[1024,128]{1,0:T(8,128)(2,1)S(1)} %bitcast.10, bf16[1024,128]{1,0:T(8,128)(2,1)S(1)} %collective-permute-done.7.other), custom_call_target="tpu_custom_call" | custom-call | tf_op jit(solution)/shard_map/pallas_call | solution.py:408
  (3 shorter events, 0.1 us)
Async XLA Ops:
  2.1 13.6 %collective-permute-start.1 = (bf16[1280,128]{1,0:T(8,128)(2,1)S(1)}, bf16[1280,128]{1,0:T(8,128)(2,1)S(1)}, u32[]{:S(2)}, u32[]{:S(2)}) collective-permute-start(bf16[1280,128]{1,0:T(8,128)(2,1)S(1)} %get-tuple-element.25.first), channel_id=1, source_target_pairs={{32,0},{64,32},{96,64},{128,96},{160,128},{192,160},{224,192},{256... | collective-permute-start | bytes 983048 | tf_op jit(solution)/shard_map/ppermute | solution.py:346
  10.9 5.9 %collective-permute-start = (bf16[1280,128]{1,0:T(8,128)(2,1)S(1)}, bf16[1280,128]{1,0:T(8,128)(2,1)S(1)}, u32[]{:S(2)}, u32[]{:S(2)}) collective-permute-start(bf16[1280,128]{1,0:T(8,128)(2,1)S(1)} %get-tuple-element.24.last), channel_id=1, source_target_pairs={{0,32},{32,64},{64,96},{96,128},{128,160},{160,192},{192,224},{224... | collective-permute-start | bytes 983048 | tf_op jit(solution)/shard_map/ppermute | solution.py:346
  18.2 11.3 %collective-permute-start.2 = (bf16[256,128]{1,0:T(8,128)(2,1)S(1)}, bf16[256,128]{1,0:T(8,128)(2,1)S(1)}, u32[]{:S(2)}, u32[]{:S(2)}) collective-permute-start(bf16[256,128]{1,0:T(8,128)(2,1)S(1)} %get-tuple-element.29.down), channel_id=1, source_target_pairs={{0,64},{32,96},{64,128},{96,160},{128,192},{160,224},{192,256},{22... | collective-permute-start | bytes 196616 | tf_op jit(solution)/shard_map/ppermute | solution.py:346
  19.5 10.0 %collective-permute-start.3 = (bf16[256,128]{1,0:T(8,128)(2,1)S(1)}, bf16[256,128]{1,0:T(8,128)(2,1)S(1)}, u32[]{:S(2)}, u32[]{:S(2)}) collective-permute-start(bf16[256,128]{1,0:T(8,128)(2,1)S(1)} %get-tuple-element.29.down), channel_id=1, source_target_pairs={{0,32},{32,64},{64,96},{96,128},{128,160},{160,192},{192,224},{224... | collective-permute-start | bytes 196616 | tf_op jit(solution)/shard_map/ppermute | solution.py:346
  24.5 5.6 %collective-permute-start.4 = (bf16[256,128]{1,0:T(8,128)(2,1)S(1)}, bf16[256,128]{1,0:T(8,128)(2,1)S(1)}, u32[]{:S(2)}, u32[]{:S(2)}) collective-permute-start(bf16[256,128]{1,0:T(8,128)(2,1)S(1)} %get-tuple-element.29.down), channel_id=1, source_target_pairs={{32,0},{64,32},{96,64},{128,96},{160,128},{192,160},{224,192},{256... | collective-permute-start | bytes 196616 | tf_op jit(solution)/shard_map/ppermute | solution.py:346
  26.4 5.5 %collective-permute-start.5 = (bf16[256,128]{1,0:T(8,128)(2,1)S(1)}, bf16[256,128]{1,0:T(8,128)(2,1)S(1)}, u32[]{:S(2)}, u32[]{:S(2)}) collective-permute-start(bf16[256,128]{1,0:T(8,128)(2,1)S(1)} %get-tuple-element.29.down), channel_id=1, source_target_pairs={{64,0},{96,32},{128,64},{160,96},{192,128},{224,160},{256,192},{28... | collective-permute-start | bytes 196616 | tf_op jit(solution)/shard_map/ppermute | solution.py:346
  38.6 4.0 %collective-permute-start.6 = (bf16[1024,128]{1,0:T(8,128)(2,1)S(1)}, bf16[1024,128]{1,0:T(8,128)(2,1)S(1)}, u32[]{:S(2)}, u32[]{:S(2)}) collective-permute-start(bf16[1024,128]{1,0:T(8,128)(2,1)S(1)} %get-tuple-element.40), channel_id=1, source_target_pairs={{0,32},{32,0},{64,96},{96,64},{128,160},{160,128},{192,224},{224,1... | collective-permute-start | bytes 786440 | tf_op jit(solution)/shard_map/ppermute | solution.py:349
  94.8 7.1 %collective-permute-start.7 = (bf16[1024,128]{1,0:T(8,128)(2,1)S(1)}, bf16[1024,128]{1,0:T(8,128)(2,1)S(1)}, u32[]{:S(2)}, u32[]{:S(2)}) collective-permute-start(bf16[1024,128]{1,0:T(8,128)(2,1)S(1)} %bitcast.9), channel_id=1, source_target_pairs={{0,32},{32,0},{64,96},{96,64},{128,160},{160,128},{192,224},{224,1... | collective-permute-start | bytes 786440 | tf_op jit(solution)/shard_map/ppermute | solution.py:349

commit v4 on v3

--- a/solution.py
+++ b/solution.py
@@ -13,6 +13,10 @@
 
 def dot(a, b, dims=NN):
     return lax.dot_general(a, b, dims, preferred_element_type=F32)
+
+
+def core():
+    return lax.axis_index("space") % 2
 
 
 def low_lanes(shape):
@@ -75,7 +79,7 @@
     return jnp.concatenate([jnp.where(low, field, swapped), jnp.where(low, swapped, field)], 0)
 
 
-def edges_kernel(volumes, cot, first, last, raw, raw_cot, planes, rows, sems):
+def edges_kernel(volumes, cot, first, last, inner, outer, raw, raw_cot, planes, rows, sems):
     copies = [pltpu.make_async_copy(volumes.at[:, x], raw.at[x], sems.at[x]) for x in range(2)]
     copies.append(pltpu.make_async_copy(cot, raw_cot, sems.at[2]))
     for copy in copies:
@@ -94,6 +98,9 @@
         block = both.T.astype(BF16)
         for out in (first, last):
             out[1024 + j * 64 : 1088 + j * 64] = block
+    even = core() == 0
+    inner[...] = jnp.where(even, last[...], first[...])
+    outer[...] = jnp.where(even, first[...], last[...])
 
 
 def prepare_kernel(
@@ -115,23 +122,22 @@
     for copy in copies:
         copy.wait()
     for dx in range(3):
-        for tz in range(4):
+        for iz in range(-1, 4):
+            if 0 <= iz < 3:
+                w = [both(w_first, dx * 9 + iy * 3 + iz) for iy in range(3)]
+                blocks = (
+                    (jnp.where(low, w[1], w[0]), jnp.where(low, w[2], w[1])),
+                    (jnp.where(low, zero, w[2]), jnp.where(low, w[0], zero)),
+                )
+            else:
+                blocks = ((zero, zero),) * 2
             for qz in range(2):
-                iz = tz - qz
-                w = [both(w_first, dx * 9 + iy * 3 + iz) for iy in range(3)] if 0 <= iz < 3 else None
-                for side in range(2):
+                tz = iz + qz
+                for side in range(2 if 0 <= tz < 4 else 0):
                     at = dx * 1024 + side * 512 + tz * 128
-                    lanes = slice(qz * 128, qz * 128 + 128)
-                    if w is None:
-                        upper = lower = zero
-                    elif side == 0:
-                        upper = jnp.where(low, w[1], w[0])
-                        lower = jnp.where(low, w[2], w[1])
-                    else:
-                        upper = jnp.where(low, zero, w[2])
-                        lower = jnp.where(low, w[0], zero)
-                    fw[at : at + 64, lanes] = upper
-                    fw[at + 64 : at + 128, lanes] = lower
+                    for half in range(2):
+                        rows = slice(at + half * 64, at + half * 64 + 64)
+                        fw[rows, qz * 128 : qz * 128 + 128] = blocks[side][half]
     for x in range(2):
         for qz in range(2):
             for qy in range(2):
@@ -142,8 +148,11 @@
         part[x * 512 : x * 512 + 512] = dot(taps[...], fw[1024 - x * 1024 : 3072 - x * 1024])
 
 
-def first_kernel(before, after, part, fw, dw, act, pre, send, taps):
+def first_kernel(outer, inner, part, fw, dw, act, pre, send, before, after, taps):
     low = low_lanes((256, 128))
+    even = core() == 0
+    before[...] = jnp.where(even, outer[...], inner[...])
+    after[...] = jnp.where(even, inner[...], outer[...])
     for x, side in enumerate((before, after)):
         gather_taps(side[0:1024], taps)
         value = part[x * 512 : x * 512 + 512] + dot(taps[...], fw[x * 2048 : x * 2048 + 1024])
@@ -201,16 +210,18 @@
 
 
 def rest_kernel(
-    core, d0, d1, d3, d4, first, last, before, after, act, slope, ct, own, acc, dw, cw, bw, out, keep, send,
+    outer, chips1, chips0, inner, first, last, before, after, act, slope, ct, own, acc, dw, cw, bw, out, keep, send,
     grads, below, above, near, taps,
 ):
     low = low_lanes((64, 128))
     for p, ref in enumerate((before, first, last, after)):
         gather_taps(ref[0:1024], taps.at[p * 512 : p * 512 + 512])
-    for p, ref in enumerate((d0, d1)):
-        gather_coarse(doubled(ref[...]), below.at[:, p * 640 : p * 640 + 640])
-    for p, ref in enumerate((d3, d4)):
-        gather_coarse(doubled(ref[...]), above.at[:, p * 640 : p * 640 + 640])
+    even, even_chip = core() == 0, lax.axis_index("space") // 2 % 2 == 0
+    i, o, a, b = inner[...], outer[...], chips0[...], chips1[...]
+    for p, plane in enumerate((jnp.where(even_chip, b, a), jnp.where(even, o, i))):
+        gather_coarse(doubled(plane), below.at[:, p * 640 : p * 640 + 640])
+    for p, plane in enumerate((jnp.where(even, i, o), jnp.where(even_chip, a, b))):
+        gather_coarse(doubled(plane), above.at[:, p * 640 : p * 640 + 640])
     pre = acc[...] + dot(below[...], cw[0:1280]) + dot(above[...], cw[1920:3200])
     s = jax.nn.sigmoid(pre)
     out[...] = (pre[:, 0:128] * s[:, 0:128]).T[64:128].astype(BF16)
@@ -270,50 +281,61 @@
         grads[at : at + 64] = (
             jnp.where(low, z1a, u0b) + pltpu.roll(jnp.where(low, z1b, u0a), 64, 1)
         ).astype(BF16)
-    here = pl.multiple_of(core[0] * 1024, 1024)
+    here = pl.multiple_of(core() * 1024, 1024)
     keep[...] = grads[pl.ds(here, 1024), :]
     send[...] = grads[pl.ds(pl.multiple_of(1024 - here, 1024), 1024), :]
 
 
-def unpack_kernel(core, mine, other, first, down, coarse, packed):
-    here = pl.multiple_of(core[0] * 1024, 1024)
+def unpack_kernel(mine, other, far_first, far_down, far_coarse, packed, first, down, coarse, sems):
+    here = pl.multiple_of(core() * 1024, 1024)
     packed[pl.ds(here, 1024), :] = mine[...]
     packed[pl.ds(pl.multiple_of(1024 - here, 1024), 1024), :] = other[...]
+    copies = []
+
+    def send(value, far):
+        copies.append(pltpu.make_async_copy(value, far, sems.at[len(copies)]))
+        copies[-1].start()
 
     def block(b):
         return packed[b * 64 : b * 64 + 64].astype(F32).T
 
-    for j in range(9):
-        dx, iz = j // 3, j % 3
-        t = block(j)
-        first[dx, 1, iz] = t[0:64]
-        first[dx, 2, iz] = t[64:128]
+    pairs = [((0, 0), (0, 2)), ((1, 0), (1, 2)), ((2, 0), (2, 2)), ((0, 1), (2, 1))]
+    t, u = block(26), block(27)
+    centers = (t[0:64], t[64:128], u[0:64])
+    for dx in range(3):
+        coarse[dx, 1, 1] = centers[dx]
+        for j in range(4):
+            t = block(14 + dx * 4 + j)
+            for h in range(2):
+                dy, dz = pairs[j][h]
+                coarse[dx, dy, dz] = t[h * 64 : h * 64 + 64]
+        send(coarse.at[dx], far_coarse.at[dx])
     for m in range(5):
         t = block(9 + m)
         for h in range(2):
             j = 2 * m + h
             if j < 9:
                 first[j // 3, 0, j % 3] = t[h * 64 : h * 64 + 64]
-    pairs = [((0, 0), (0, 2)), ((1, 0), (1, 2)), ((2, 0), (2, 2)), ((0, 1), (2, 1))]
     for dx in range(3):
-        for j in range(4):
-            t = block(14 + dx * 4 + j)
-            for h in range(2):
-                dy, dz = pairs[j][h]
-                coarse[dx, dy, dz] = t[h * 64 : h * 64 + 64]
-    t = block(26)
-    coarse[0, 1, 1] = t[0:64]
-    coarse[1, 1, 1] = t[64:128]
-    coarse[2, 1, 1] = block(27)[0:64]
+        for iz in range(3):
+            t = block(dx * 3 + iz)
+            first[dx, 1, iz] = t[0:64]
+            first[dx, 2, iz] = t[64:128]
+        send(first.at[dx], far_first.at[dx])
     for j in range(4):
         t = block(28 + j)
         for qy in range(2):
             down[j // 2, qy, j % 2] = t[qy * 64 : qy * 64 + 64]
-
-
-def call(kernel, outs, scratch=(), places=""):
-    kinds = {"s": pltpu.SMEM, "h": pltpu.HBM, "v": pltpu.VMEM}
+    send(down, far_down)
+    for copy in copies:
+        copy.wait()
+
+
+def call(kernel, outs, scratch=(), places="", home=""):
+    kinds = {"h": pltpu.HBM, "v": pltpu.VMEM}
     specs = {"in_specs": [pl.BlockSpec(memory_space=kinds[p]) for p in places]} if places else {}
+    if home:
+        specs["out_specs"] = [pl.BlockSpec(memory_space=kinds[p]) for p in home]
     return pl.pallas_call(
         kernel,
         out_shape=[jax.ShapeDtypeStruct(s, d) for s, d in outs],
@@ -341,16 +363,15 @@
 def local(volumes, w_first, w_down, w_coarse, cotangent):
     n, m = lax.axis_size("space"), lax.axis_size("dp")
 
-    def shift(value, by):
-        steps = [(i, i + by) for i in range(n) if 0 <= i + by < n]
-        return lax.ppermute(value, "space", steps)
-
-    def partner(value):
-        return lax.ppermute(value, "space", [(i, i ^ 1) for i in range(n)])
-
-    first, last = call(
+    def swap(value, pairs):
+        return lax.ppermute(value, "space", [p for i, j in pairs for p in ((i, j), (j, i))])
+
+    chip = [(i, i + 1) for i in range(0, n, 2)]
+    across = [(i, i + 1) for i in range(1, n - 1, 2)]
+    beside = [[(i, i + 2) for i in range(n - 2) if i // 2 % 2 == k] for k in range(2)]
+    first, last, inner, outer = call(
         edges_kernel,
-        [((1280, 128), BF16)] * 2,
+        [((1280, 128), BF16)] * 4,
         [
             ((2, 64, 16, 128), BF16),
             ((64, 8, 64), BF16),
@@ -360,20 +381,20 @@
         ],
         "hh",
     )(far(volumes.reshape(64, 2, 16, 128)), far(cotangent.reshape(64, 8, 64)))
-    before = shift(last, 1)
-    after = shift(first, -1)
+    inner, outer = swap(inner, chip), swap(outer, across)
     part, fw, dw = call(
         prepare_kernel,
         [((1024, 256), F32), ((3072, 256), BF16), ((512, 128), BF16)],
         [((512, 2048), BF16), ((1728, 64), BF16), ((512, 64), BF16), pltpu.SemaphoreType.DMA((2,))],
         "vvhh",
     )(first, last, far(w_first.reshape(1728, 64)), far(w_down.reshape(512, 64)))
-    act, pre, down = call(
+    act, pre, down, before, after = call(
         first_kernel,
-        [((512, 512), BF16), ((1024, 256), F32), ((256, 128), BF16)],
+        [((512, 512), BF16), ((1024, 256), F32), ((256, 128), BF16)] + [((1280, 128), BF16)] * 2,
         [((512, 1024), BF16)],
-    )(before, after, part, fw, dw)
-    halo = [shift(down, 2), shift(down, 1), shift(down, -1), shift(down, -2)]
+        "vvvvv",
+    )(outer, inner, part, fw, dw)
+    halo = [swap(down, pairs) for pairs in (across, beside[1], beside[0], chip)]
     cw, bw, slope, ct, own, acc = call(
         beside_kernel,
         [
@@ -387,7 +408,6 @@
         [((1728, 64), BF16), pltpu.SemaphoreType.DMA],
         "vvvvvh",
     )(first, before, after, pre, down, far(w_coarse.reshape(1728, 64)))
-    core = lax.rem(lax.axis_index("space"), 2).reshape(1)
     out, keep, send = call(
         rest_kernel,
         [((64, 512), BF16), ((1024, 128), BF16), ((1024, 128), BF16)],
@@ -398,9 +418,9 @@
             ((512, 1920), BF16),
             ((2048, 1024), BF16),
         ],
-        "s" + 16 * "v",
-    )(core, *halo, first, last, before, after, act, slope, ct, own, acc, dw, cw, bw)
-    half = (keep.astype(F32) + partner(send).astype(F32)).astype(BF16)
+        16 * "v",
+    )(*halo, first, last, before, after, act, slope, ct, own, acc, dw, cw, bw)
+    half = (keep.astype(F32) + swap(send, chip).astype(F32)).astype(BF16)
     chips = [list(range(c, n, 2)) for c in range(2)]
     piece = scatter_sum(half, "dp", m)
     piece = jnp.sum(spread(piece, "space", n // 2, chips).astype(F32), 0).astype(BF16)
@@ -408,9 +428,16 @@
     grad_first, grad_down, grad_coarse = call(
         unpack_kernel,
         [((3, 3, 3, 64, 64), F32), ((2, 2, 2, 64, 64), F32), ((3, 3, 3, 64, 64), F32)],
-        [((2048, 128), BF16)],
-        "svv",
-    )(core, mine, partner(mine))
+        [
+            ((2048, 128), BF16),
+            ((3, 3, 3, 64, 64), F32),
+            ((2, 2, 2, 64, 64), F32),
+            ((3, 3, 3, 64, 64), F32),
+            pltpu.SemaphoreType.DMA((7,)),
+        ],
+        "vv",
+        "hhh",
+    )(mine, swap(mine, chip))
     return (out.reshape(1, 64, 1, 8, 64), grad_first, grad_down, grad_coarse)
 
 

time: 104 us -> 99.8 us (0.960)
  waiting for transfers between devices: 4.99 us -> 1.51 us
  blocking collectives: 52.1 us -> 48.9 us
  starting transfers between devices: 29 us -> 31.2 us
    all_to_all x2, blocking collectives: 31.6 us -> 27.9 us  [spread(): return lax.all_to_all(y, axis, 0, 0, tiled=True, axis_index_groups=groups)]
    ppermute x8, waiting for transfers between devices: 4.99 us -> 1.51 us  [swap(): lax.ppermute(value, 'space', [p for i, j in pairs for p in ((i, j), (j, i...]
    ppermute x8, starting transfers between devices: 29 us -> 31.2 us  [swap(): lax.ppermute(value, 'space', [p for i, j in pairs for p in ((i, j), (j, i...]
  transfers between devices with their start and end apart: 8 -> 8, of which waited for: 5 -> 2; matrix products, arithmetic and copies ran while one was open for 1% -> 1% of each run, Pallas kernels for 4% -> 5%
where the time goes in v4:
time: 99.8 us; the launch traced here: 99.3 us
  blocking collectives  48.9 us (49%)
  starting transfers between devices  31.2 us (31%)
  Pallas kernels  15.9 us (16%)
  waiting for transfers between devices  1.51 us (2%)
    ppermute x8, starting transfers between devices, swap(): lax.ppermute(value, 'space', [p for i, j in pairs for p in ((i, j), (j, i...  31.2 us
    all_to_all x2, blocking collectives, spread(): return lax.all_to_all(y, axis, 0, 0, tiled=True, axis_index_groups=groups)  27.9 us
    all_to_all x1, blocking collectives, scatter_sum(): y = lax.all_to_all(y, axis, 0, 0, tiled=True, axis_index_groups=groups)  21 us
    pallas_call x1, Pallas kernels, local(): call(rest_kernel, [((64, 512), BF16), ((1024, 128), BF16), ((1024, 128),...  6.78 us
    pallas_call x1, Pallas kernels, local(): call(prepare_kernel, [((1024, 256), F32), ((3072, 256), BF16), ((512, 128...  2.81 us
  transfers between devices with their start and end apart: 8, of which 2 were waited for; matrix products, arithmetic and copies ran while one was open for 1% of the time, Pallas kernels for 5%

profile of v4, /device:TPU:1, one launch (start us, length us, event | category | flops | bytes accessed | tf_op | source)
XLA Modules:
  0.0 99.3 jit_solution(11225496002984415836)
XLA Ops:
  0.6 1.6 %shard_map.84 = (bf16[1280,128]{1,0:T(8,128)(2,1)S(1)}, bf16[1280,128]{1,0:T(8,128)(2,1)S(1)}, bf16[1280,128]{1,0:T(8,128)(2,1)S(1)}, bf16[1280,128]{1,0:T(8,128)(2,1)S(1)}) custom-call(bf16[64,2,16,128]{3,2,1,0:T(8,128)(2,1)} %bitcast.11, bf16[64,8,64]{2,1,0:T(8,128)(2,1)} %bitcast.14), custom_call_target="tpu_custom_call" | custom-call | tf_op jit(solution)/shard_map/pallas_call | solution.py:372
  2.3 5.4 %collective-permute-start = (bf16[1280,128]{1,0:T(8,128)(2,1)S(1)}, bf16[1280,128]{1,0:T(8,128)(2,1)S(1)}, u32[]{:S(2)}, u32[]{:S(2)}) collective-permute-start(bf16[1280,128]{1,0:T(8,128)(2,1)S(1)} %get-tuple-element.28), channel_id=1, source_target_pairs={{32,64},{64,32},{96,128},{128,96},{160,192},{192,160},{224,256},{2... | collective-permute-start | bytes 983048 | tf_op jit(solution)/shard_map/ppermute | solution.py:367
  7.7 4.1 %collective-permute-start.1 = (bf16[1280,128]{1,0:T(8,128)(2,1)S(1)}, bf16[1280,128]{1,0:T(8,128)(2,1)S(1)}, u32[]{:S(2)}, u32[]{:S(2)}) collective-permute-start(bf16[1280,128]{1,0:T(8,128)(2,1)S(1)} %get-tuple-element.29), channel_id=1, source_target_pairs={{0,32},{32,0},{64,96},{96,64},{128,160},{160,128},{192,224},{224,1... | collective-permute-start | bytes 983048 | tf_op jit(solution)/shard_map/ppermute | solution.py:367
  11.8 2.8 %shard_map.85 = (f32[1024,256]{1,0:T(8,128)S(1)}, bf16[3072,256]{1,0:T(8,128)(2,1)S(1)}, bf16[512,128]{1,0:T(8,128)(2,1)S(1)}) custom-call(bf16[1280,128]{1,0:T(8,128)(2,1)S(1)} %get-tuple-element.30.first, bf16[1280,128]{1,0:T(8,128)(2,1)S(1)} %get-tuple-element.31.last, bf16[1728,64]{1,0:T(8,128)(2,1)} %bitcast.12, bf16[512,64]{1,0:T(8,128)(2,1)} %bitcast.15), custom_call_target="tpu_custom_call" | custom-call | tf_op jit(solution)/shard_map/pallas_call | solution.py:385
  14.6 0.0 collective-permute-done.outer
  14.6 0.0 collective-permute-done.1.inner
  14.6 1.4 %shard_map.86 = (bf16[512,512]{1,0:T(8,128)(2,1)S(1)}, f32[1024,256]{1,0:T(8,128)S(1)}, bf16[256,128]{1,0:T(8,128)(2,1)S(1)}, bf16[1280,128]{1,0:T(8,128)(2,1)S(1)}, bf16[1280,128]{1,0:T(8,128)(2,1)S(1)}) custom-call(bf16[1280,128]{1,0:T(8,128)(2,1)S(1)} %collective-permute-done.outer, bf16[1280,128]{1,0:T(8,128)(2,1)S(1)} %collective-permute-done.1.inner, ...), custom_call_target="tpu_custom_call" | custom-call | tf_op jit(solution)/shard_map/pallas_call | solution.py:391
  16.0 2.2 %collective-permute-start.2 = (bf16[256,128]{1,0:T(8,128)(2,1)S(1)}, bf16[256,128]{1,0:T(8,128)(2,1)S(1)}, u32[]{:S(2)}, u32[]{:S(2)}) collective-permute-start(bf16[256,128]{1,0:T(8,128)(2,1)S(1)} %get-tuple-element.35.down), channel_id=1, source_target_pairs={{32,64},{64,32},{96,128},{128,96},{160,192},{192,160},{224,256},{2... | collective-permute-start | bytes 196616 | tf_op jit(solution)/shard_map/ppermute | solution.py:367
  18.2 0.7 collective-permute-start.3
  18.9 8.6 %collective-permute-start.4 = (bf16[256,128]{1,0:T(8,128)(2,1)S(1)}, bf16[256,128]{1,0:T(8,128)(2,1)S(1)}, u32[]{:S(2)}, u32[]{:S(2)}) collective-permute-start(bf16[256,128]{1,0:T(8,128)(2,1)S(1)} %get-tuple-element.35.down), channel_id=1, source_target_pairs={{0,64},{64,0},{32,96},{96,32},{128,192},{192,128},{160,224},{224,1... | collective-permute-start | bytes 196616 | tf_op jit(solution)/shard_map/ppermute | solution.py:367
  27.4 1.9 %collective-permute-start.5 = (bf16[256,128]{1,0:T(8,128)(2,1)S(1)}, bf16[256,128]{1,0:T(8,128)(2,1)S(1)}, u32[]{:S(2)}, u32[]{:S(2)}) collective-permute-start(bf16[256,128]{1,0:T(8,128)(2,1)S(1)} %get-tuple-element.35.down), channel_id=1, source_target_pairs={{0,32},{32,0},{64,96},{96,64},{128,160},{160,128},{192,224},{224,1... | collective-permute-start | bytes 196616 | tf_op jit(solution)/shard_map/ppermute | solution.py:367
  29.4 1.8 %shard_map.87 = (bf16[3200,256]{1,0:T(8,128)(2,1)S(1)}, bf16[64,1920]{1,0:T(8,128)(2,1)S(1)}, f32[1024,256]{1,0:T(8,128)S(1)}, f32[512,256]{1,0:T(8,128)S(1)}, b...) custom-call(bf16[1280,128]{1,0:T(8,128)(2,1)S(1)} %get-tuple-element.30.first, ...), custom_call_target="tpu_custom_call" | custom-call | tf_op jit(solution)/shard_map/pallas_call | solution.py:398
  31.1 0.0 collective-permute-done.2.outer
  31.2 0.0 collective-permute-done.3.chips1
  31.2 0.0 collective-permute-done.4.chips0
  31.2 0.0 collective-permute-done.5.inner
  31.2 6.8 %shard_map.88 = (bf16[64,512]{1,0:T(8,128)(2,1)S(1)}, bf16[1024,128]{1,0:T(8,128)(2,1)S(1)}, bf16[1024,128]{1,0:T(8,128)(2,1)S(1)}) custom-call(bf16[256,128]{1,0:T(8,128)(2,1)S(1)} %collective-permute-done.2.outer, bf16[256,128]{1,0:T(8,128)(2,1)S(1)} %collective-permute-done.3.chips1, bf16[256,128]{1,0:T(8,128)(2,1)S(1)} %collective-permute-done.4.chips0, ...), custom_call_target="tpu_custom_call" | custom-call | tf_op jit(solution)/shard_map/pallas_call | solution.py:411
  38.0 2.4 %collective-permute-start.6 = (bf16[1024,128]{1,0:T(8,128)(2,1)S(1)}, bf16[1024,128]{1,0:T(8,128)(2,1)S(1)}, u32[]{:S(2)}, u32[]{:S(2)}) collective-permute-start(bf16[1024,128]{1,0:T(8,128)(2,1)S(1)} %get-tuple-element.48), channel_id=1, source_target_pairs={{0,32},{32,0},{64,96},{96,64},{128,160},{160,128},{192,224},{224,1... | collective-permute-start | bytes 786440 | tf_op jit(solution)/shard_map/ppermute | solution.py:367
  40.4 1.1 %collective-permute-done.6 = bf16[1024,128]{1,0:T(8,128)(2,1)S(1)} collective-permute-done((bf16[1024,128]{1,0:T(8,128)(2,1)S(1)}, bf16[1024,128]{1,0:T(8,128)(2,1)S(1)}, u32[]{:S(2)}, u32[]{:S(2)}) %collective-permute-start.6) | collective-permute-done | bytes 262176 | tf_op jit(solution)/shard_map/ppermute | solution.py:367
  41.5 0.1 add_convert_fusion
  41.6 21.0 %all_to_all.15 = bf16[32,32,128]{2,1,0:T(8,128)(2,1)S(1)} all-to-all(bf16[32,32,128]{2,1,0:T(8,128)(2,1)S(1)} %bitcast.10), channel_id=1, replica_groups=mesh['space'=16,'dp'=32] {'dp'}, dimensions={0} | all-to-all | bytes 524288 | tf_op jit(solution)/shard_map/all_to_all | solution.py:354
  62.6 0.1 reduce_sum.24
  62.7 13.0 %all_to_all.16 = bf16[8,32,128]{2,1,0:T(8,128)(2,1)S(1)} all-to-all(bf16[8,32,128]{2,1,0:T(8,128)(2,1)S(1)} %broadcast_in_dim.4), channel_id=1, replica_groups={{0,64,128,192,256,320,384,448},{32,96,160,224,288,352,416,480},{1,65,12..., dimensions={0} | all-to-all | bytes 131072 | tf_op jit(solution)/shard_map/all_to_all | solution.py:360
  75.7 15.0 %all_to_all.17 = bf16[32,32,128]{2,1,0:T(8,128)(2,1)S(1)} all-to-all(bf16[32,32,128]{2,1,0:T(8,128)(2,1)S(1)} %broadcast_in_dim.5), channel_id=1, replica_groups=mesh['space'=16,'dp'=32] {'dp'}, dimensions={0} | all-to-all | bytes 524288 | tf_op jit(solution)/shard_map/all_to_all | solution.py:360
  90.7 6.0 %collective-permute-start.7 = (bf16[1024,128]{1,0:T(8,128)(2,1)S(1)}, bf16[1024,128]{1,0:T(8,128)(2,1)S(1)}, u32[]{:S(2)}, u32[]{:S(2)}) collective-permute-start(bf16[1024,128]{1,0:T(8,128)(2,1)S(1)} %bitcast.8), channel_id=1, source_target_pairs={{0,32},{32,0},{64,96},{96,64},{128,160},{160,128},{192,224},{224,1... | collective-permute-start | bytes 786440 | tf_op jit(solution)/shard_map/ppermute | solution.py:367
  96.7 0.8 reshape.39
  97.4 0.4 collective-permute-done.7.other
  97.8 1.5 %shard_map.89 = (f32[3,3,3,64,64]{4,3,2,1,0:T(8,128)}, f32[2,2,2,64,64]{4,3,2,1,0:T(8,128)}, f32[3,3,3,64,64]{4,3,2,1,0:T(8,128)}) custom-call(bf16[1024,128]{1,0:T(8,128)(2,1)S(1)} %bitcast.9, bf16[1024,128]{1,0:T(8,128)(2,1)S(1)} %collective-permute-done.7.other), custom_call_target="tpu_custom_call" | custom-call | tf_op jit(solution)/shard_map/pallas_call | solution.py:428
  (3 shorter events, 0.1 us)
Async XLA Ops:
  2.3 12.3 %collective-permute-start = (bf16[1280,128]{1,0:T(8,128)(2,1)S(1)}, bf16[1280,128]{1,0:T(8,128)(2,1)S(1)}, u32[]{:S(2)}, u32[]{:S(2)}) collective-permute-start(bf16[1280,128]{1,0:T(8,128)(2,1)S(1)} %get-tuple-element.28), channel_id=1, source_target_pairs={{32,64},{64,32},{96,128},{128,96},{160,192},{192,160},{224,256},{2... | collective-permute-start | bytes 983048 | tf_op jit(solution)/shard_map/ppermute | solution.py:367
  7.7 6.9 %collective-permute-start.1 = (bf16[1280,128]{1,0:T(8,128)(2,1)S(1)}, bf16[1280,128]{1,0:T(8,128)(2,1)S(1)}, u32[]{:S(2)}, u32[]{:S(2)}) collective-permute-start(bf16[1280,128]{1,0:T(8,128)(2,1)S(1)} %get-tuple-element.29), channel_id=1, source_target_pairs={{0,32},{32,0},{64,96},{96,64},{128,160},{160,128},{192,224},{224,1... | collective-permute-start | bytes 983048 | tf_op jit(solution)/shard_map/ppermute | solution.py:367
  16.0 15.2 %collective-permute-start.2 = (bf16[256,128]{1,0:T(8,128)(2,1)S(1)}, bf16[256,128]{1,0:T(8,128)(2,1)S(1)}, u32[]{:S(2)}, u32[]{:S(2)}) collective-permute-start(bf16[256,128]{1,0:T(8,128)(2,1)S(1)} %get-tuple-element.35.down), channel_id=1, source_target_pairs={{32,64},{64,32},{96,128},{128,96},{160,192},{192,160},{224,256},{2... | collective-permute-start | bytes 196616 | tf_op jit(solution)/shard_map/ppermute | solution.py:367
  18.2 12.9 %collective-permute-start.3 = (bf16[256,128]{1,0:T(8,128)(2,1)S(1)}, bf16[256,128]{1,0:T(8,128)(2,1)S(1)}, u32[]{:S(2)}, u32[]{:S(2)}) collective-permute-start(bf16[256,128]{1,0:T(8,128)(2,1)S(1)} %get-tuple-element.35.down), channel_id=1, source_target_pairs={{64,128},{128,64},{96,160},{160,96},{192,256},{256,192},{224,288},... | collective-permute-start | bytes 196616 | tf_op jit(solution)/shard_map/ppermute | solution.py:367
  18.9 12.3 %collective-permute-start.4 = (bf16[256,128]{1,0:T(8,128)(2,1)S(1)}, bf16[256,128]{1,0:T(8,128)(2,1)S(1)}, u32[]{:S(2)}, u32[]{:S(2)}) collective-permute-start(bf16[256,128]{1,0:T(8,128)(2,1)S(1)} %get-tuple-element.35.down), channel_id=1, source_target_pairs={{0,64},{64,0},{32,96},{96,32},{128,192},{192,128},{160,224},{224,1... | collective-permute-start | bytes 196616 | tf_op jit(solution)/shard_map/ppermute | solution.py:367
  27.4 3.7 %collective-permute-start.5 = (bf16[256,128]{1,0:T(8,128)(2,1)S(1)}, bf16[256,128]{1,0:T(8,128)(2,1)S(1)}, u32[]{:S(2)}, u32[]{:S(2)}) collective-permute-start(bf16[256,128]{1,0:T(8,128)(2,1)S(1)} %get-tuple-element.35.down), channel_id=1, source_target_pairs={{0,32},{32,0},{64,96},{96,64},{128,160},{160,128},{192,224},{224,1... | collective-permute-start | bytes 196616 | tf_op jit(solution)/shard_map/ppermute | solution.py:367
  38.0 3.6 %collective-permute-start.6 = (bf16[1024,128]{1,0:T(8,128)(2,1)S(1)}, bf16[1024,128]{1,0:T(8,128)(2,1)S(1)}, u32[]{:S(2)}, u32[]{:S(2)}) collective-permute-start(bf16[1024,128]{1,0:T(8,128)(2,1)S(1)} %get-tuple-element.48), channel_id=1, source_target_pairs={{0,32},{32,0},{64,96},{96,64},{128,160},{160,128},{192,224},{224,1... | collective-permute-start | bytes 786440 | tf_op jit(solution)/shard_map/ppermute | solution.py:367
  90.7 7.1 %collective-permute-start.7 = (bf16[1024,128]{1,0:T(8,128)(2,1)S(1)}, bf16[1024,128]{1,0:T(8,128)(2,1)S(1)}, u32[]{:S(2)}, u32[]{:S(2)}) collective-permute-start(bf16[1024,128]{1,0:T(8,128)(2,1)S(1)} %bitcast.8), channel_id=1, source_target_pairs={{0,32},{32,0},{64,96},{96,64},{128,160},{160,128},{192,224},{224,1... | collective-permute-start | bytes 786440 | tf_op jit(solution)/shard_map/ppermute | solution.py:367

commit v5 on v4

--- a/solution.py
+++ b/solution.py
@@ -104,7 +104,7 @@
 
 
 def prepare_kernel(
-    first, last, far_first, far_down, part, fw, dw, taps, w_first, w_down, sems
+    first, last, far_first, far_down, part, fw, dw, taps, w_first, w_down, wide_first, wide_down, sems
 ):
     weights = ((far_first, w_first), (far_down, w_down))
     copies = [pltpu.make_async_copy(far, to, sems.at[i]) for i, (far, to) in enumerate(weights)]
@@ -115,16 +115,18 @@
     pair = twice()
 
     def both(ref, k):
-        return dot(ref[k * 64 : k * 64 + 64], pair).astype(BF16)
+        return ref[k * 64 : k * 64 + 64]
 
     for x, ref in enumerate((first, last)):
         gather_taps(ref[0:1024], taps.at[:, x * 1024 : x * 1024 + 1024])
     for copy in copies:
         copy.wait()
+    wide_first[...] = dot(w_first[...], pair).astype(BF16)
+    wide_down[...] = dot(w_down[...], pair).astype(BF16)
     for dx in range(3):
         for iz in range(-1, 4):
             if 0 <= iz < 3:
-                w = [both(w_first, dx * 9 + iy * 3 + iz) for iy in range(3)]
+                w = [both(wide_first, dx * 9 + iy * 3 + iz) for iy in range(3)]
                 blocks = (
                     (jnp.where(low, w[1], w[0]), jnp.where(low, w[2], w[1])),
                     (jnp.where(low, zero, w[2]), jnp.where(low, w[0], zero)),
@@ -143,12 +145,12 @@
             for qy in range(2):
                 k = x * 4 + qy * 2 + qz
                 at = (x * 4 + qz * 2 + qy) * 64
-                dw[at : at + 64] = both(w_down, k)
+                dw[at : at + 64] = both(wide_down, k)
     for x in range(2):
         part[x * 512 : x * 512 + 512] = dot(taps[...], fw[1024 - x * 1024 : 3072 - x * 1024])
 
 
-def first_kernel(outer, inner, part, fw, dw, act, pre, send, before, after, taps):
+def first_kernel(outer, inner, part, fw, dw, act, slope, send, before, after, taps):
     low = low_lanes((256, 128))
     even = core() == 0
     before[...] = jnp.where(even, outer[...], inner[...])
@@ -156,20 +158,18 @@
     for x, side in enumerate((before, after)):
         gather_taps(side[0:1024], taps)
         value = part[x * 512 : x * 512 + 512] + dot(taps[...], fw[x * 2048 : x * 2048 + 1024])
-        pre[x * 512 : x * 512 + 512] = value
-        act[:, x * 256 : x * 256 + 256] = (value * jax.nn.sigmoid(value)).astype(BF16)
+        s = jax.nn.sigmoid(value)
+        slope[x * 512 : x * 512 + 512] = s * (1.0 + value * (1.0 - s))
+        act[:, x * 256 : x * 256 + 256] = (value * s).astype(BF16)
     down = dot(act[...], dw[...])
     send[...] = jnp.where(low, down[:256], down[256:]).astype(BF16)
 
 
 def beside_kernel(
-    first, before, after, pre, down, far_coarse, cw, bw, slope, ct, own, acc, w_coarse, sem
+    first, before, after, down, far_coarse, cw, bw, ct, own, acc, w_coarse, wide, sem
 ):
     copy = pltpu.make_async_copy(far_coarse, w_coarse, sem)
     copy.start()
-    value = pre[...]
-    s = jax.nn.sigmoid(value)
-    slope[...] = s * (1.0 + value * (1.0 - s))
     low = low_lanes((256, 128))
     f0, t0 = turned(before[1024:1280])
     f1, t1 = turned(first[1024:1280])
@@ -184,15 +184,16 @@
     pair = twice()
 
     def both(ref, k):
-        return dot(ref[k * 64 : k * 64 + 64], pair).astype(BF16)
+        return ref[k * 64 : k * 64 + 64]
 
     copy.wait()
+    wide[...] = dot(w_coarse[...], pair).astype(BF16)
     order = [(0, 0), (0, 2), (1, 0), (1, 2), (2, 0), (2, 2), (0, 1), (2, 1), (1, 1), None]
     for j, tap in enumerate(order):
         if tap is None:
             w = [zero] * 3
         else:
-            w = [both(w_coarse, dx * 9 + tap[0] * 3 + tap[1]) for dx in range(3)]
+            w = [both(wide, dx * 9 + tap[0] * 3 + tap[1]) for dx in range(3)]
         w = [zero] * 2 + w + [zero] * 2
         for p in range(5):
             at = p * 640 + j * 64
@@ -200,7 +201,7 @@
             cw[at : at + 64, 128:256] = jnp.where(low, w[p], zero)
     for dx in range(3):
         back = [
-            zero if tap is None else both(w_coarse, (2 - dx) * 9 + (2 - tap[0]) * 3 + 2 - tap[1])
+            zero if tap is None else both(wide, (2 - dx) * 9 + (2 - tap[0]) * 3 + 2 - tap[1])
             for tap in order
         ]
         for j in range(5):
@@ -385,29 +386,35 @@
     part, fw, dw = call(
         prepare_kernel,
         [((1024, 256), F32), ((3072, 256), BF16), ((512, 128), BF16)],
-        [((512, 2048), BF16), ((1728, 64), BF16), ((512, 64), BF16), pltpu.SemaphoreType.DMA((2,))],
+        [
+            ((512, 2048), BF16),
+            ((1728, 64), BF16),
+            ((512, 64), BF16),
+            ((1728, 128), BF16),
+            ((512, 128), BF16),
+            pltpu.SemaphoreType.DMA((2,)),
+        ],
         "vvhh",
     )(first, last, far(w_first.reshape(1728, 64)), far(w_down.reshape(512, 64)))
-    act, pre, down, before, after = call(
+    act, slope, down, before, after = call(
         first_kernel,
         [((512, 512), BF16), ((1024, 256), F32), ((256, 128), BF16)] + [((1280, 128), BF16)] * 2,
         [((512, 1024), BF16)],
         "vvvvv",
     )(outer, inner, part, fw, dw)
     halo = [swap(down, pairs) for pairs in (across, beside[1], beside[0], chip)]
-    cw, bw, slope, ct, own, acc = call(
+    cw, bw, ct, own, acc = call(
         beside_kernel,
         [
             ((3200, 256), BF16),
             ((64, 1920), BF16),
-            ((1024, 256), F32),
             ((512, 256), F32),
             ((512, 640), BF16),
             ((512, 256), F32),
         ],
-        [((1728, 64), BF16), pltpu.SemaphoreType.DMA],
-        "vvvvvh",
-    )(first, before, after, pre, down, far(w_coarse.reshape(1728, 64)))
+        [((1728, 64), BF16), ((1728, 128), BF16), pltpu.SemaphoreType.DMA],
+        "vvvvh",
+    )(first, before, after, down, far(w_coarse.reshape(1728, 64)))
     out, keep, send = call(
         rest_kernel,
         [((64, 512), BF16), ((1024, 128), BF16), ((1024, 128), BF16)],

time: 99.8 us -> 100 us (level)
  no operation moved by 1% of the time
where the time goes in v5:
time: 100 us; the launch traced here: 99.7 us
  blocking collectives  48.5 us (48%)
  starting transfers between devices  31.3 us (31%)
  Pallas kernels  16.3 us (16%)
  waiting for transfers between devices  1.87 us (2%)
    ppermute x8, starting transfers between devices, swap(): lax.ppermute(value, 'space', [p for i, j in pairs for p in ((i, j), (j, i...  31.3 us
    all_to_all x2, blocking collectives, spread(): return lax.all_to_all(y, axis, 0, 0, tiled=True, axis_index_groups=groups)  27.2 us
    all_to_all x1, blocking collectives, scatter_sum(): y = lax.all_to_all(y, axis, 0, 0, tiled=True, axis_index_groups=groups)  21.3 us
    pallas_call x1, Pallas kernels, local(): call(rest_kernel, [((64, 512), BF16), ((1024, 128), BF16), ((1024, 128),...  6.79 us
    pallas_call x1, Pallas kernels, local(): call(prepare_kernel, [((1024, 256), F32), ((3072, 256), BF16), ((512, 128...  2.96 us
  transfers between devices with their start and end apart: 8, of which 2 were waited for; matrix products, arithmetic and copies ran while one was open for 1% of the time, Pallas kernels for 5%

profile of v5, /device:TPU:1, one launch (start us, length us, event | category | flops | bytes accessed | tf_op | source)
XLA Modules:
  0.0 99.7 jit_solution(7677243499288579702)
XLA Ops:
  0.6 1.6 %shard_map.84 = (bf16[1280,128]{1,0:T(8,128)(2,1)S(1)}, bf16[1280,128]{1,0:T(8,128)(2,1)S(1)}, bf16[1280,128]{1,0:T(8,128)(2,1)S(1)}, bf16[1280,128]{1,0:T(8,128)(2,1)S(1)}) custom-call(bf16[64,2,16,128]{3,2,1,0:T(8,128)(2,1)} %bitcast.11, bf16[64,8,64]{2,1,0:T(8,128)(2,1)} %bitcast.14), custom_call_target="tpu_custom_call" | custom-call | tf_op jit(solution)/shard_map/pallas_call | solution.py:373
  2.3 5.4 %collective-permute-start = (bf16[1280,128]{1,0:T(8,128)(2,1)S(1)}, bf16[1280,128]{1,0:T(8,128)(2,1)S(1)}, u32[]{:S(2)}, u32[]{:S(2)}) collective-permute-start(bf16[1280,128]{1,0:T(8,128)(2,1)S(1)} %get-tuple-element.27), channel_id=1, source_target_pairs={{32,64},{64,32},{96,128},{128,96},{160,192},{192,160},{224,256},{2... | collective-permute-start | bytes 983048 | tf_op jit(solution)/shard_map/ppermute | solution.py:368
  7.7 4.1 %collective-permute-start.1 = (bf16[1280,128]{1,0:T(8,128)(2,1)S(1)}, bf16[1280,128]{1,0:T(8,128)(2,1)S(1)}, u32[]{:S(2)}, u32[]{:S(2)}) collective-permute-start(bf16[1280,128]{1,0:T(8,128)(2,1)S(1)} %get-tuple-element.28), channel_id=1, source_target_pairs={{0,32},{32,0},{64,96},{96,64},{128,160},{160,128},{192,224},{224,1... | collective-permute-start | bytes 983048 | tf_op jit(solution)/shard_map/ppermute | solution.py:368
  11.8 3.0 %shard_map.85 = (f32[1024,256]{1,0:T(8,128)S(1)}, bf16[3072,256]{1,0:T(8,128)(2,1)S(1)}, bf16[512,128]{1,0:T(8,128)(2,1)S(1)}) custom-call(bf16[1280,128]{1,0:T(8,128)(2,1)S(1)} %get-tuple-element.29.first, bf16[1280,128]{1,0:T(8,128)(2,1)S(1)} %get-tuple-element.30.last, bf16[1728,64]{1,0:T(8,128)(2,1)} %bitcast.12, bf16[512,64]{1,0:T(8,128)(2,1)} %bitcast.15), custom_call_target="tpu_custom_call" | custom-call | tf_op jit(solution)/shard_map/pallas_call | solution.py:386
  14.7 0.0 collective-permute-done.outer
  14.7 0.0 collective-permute-done.1.inner
  14.7 1.4 %shard_map.86 = (bf16[512,512]{1,0:T(8,128)(2,1)S(1)}, f32[1024,256]{1,0:T(8,128)S(1)}, bf16[256,128]{1,0:T(8,128)(2,1)S(1)}, bf16[1280,128]{1,0:T(8,128)(2,1)S(1)}, bf16[1280,128]{1,0:T(8,128)(2,1)S(1)}) custom-call(bf16[1280,128]{1,0:T(8,128)(2,1)S(1)} %collective-permute-done.outer, bf16[1280,128]{1,0:T(8,128)(2,1)S(1)} %collective-permute-done.1.inner, ...), custom_call_target="tpu_custom_call" | custom-call | tf_op jit(solution)/shard_map/pallas_call | solution.py:399
  16.2 1.9 %collective-permute-start.5 = (bf16[256,128]{1,0:T(8,128)(2,1)S(1)}, bf16[256,128]{1,0:T(8,128)(2,1)S(1)}, u32[]{:S(2)}, u32[]{:S(2)}) collective-permute-start(bf16[256,128]{1,0:T(8,128)(2,1)S(1)} %get-tuple-element.34.down), channel_id=1, source_target_pairs={{0,32},{32,0},{64,96},{96,64},{128,160},{160,128},{192,224},{224,1... | collective-permute-start | bytes 196616 | tf_op jit(solution)/shard_map/ppermute | solution.py:368
  18.1 2.3 %collective-permute-start.4 = (bf16[256,128]{1,0:T(8,128)(2,1)S(1)}, bf16[256,128]{1,0:T(8,128)(2,1)S(1)}, u32[]{:S(2)}, u32[]{:S(2)}) collective-permute-start(bf16[256,128]{1,0:T(8,128)(2,1)S(1)} %get-tuple-element.34.down), channel_id=1, source_target_pairs={{0,64},{64,0},{32,96},{96,32},{128,192},{192,128},{160,224},{224,1... | collective-permute-start | bytes 196616 | tf_op jit(solution)/shard_map/ppermute | solution.py:368
  20.4 0.7 collective-permute-start.3
  21.1 9.0 %collective-permute-start.2 = (bf16[256,128]{1,0:T(8,128)(2,1)S(1)}, bf16[256,128]{1,0:T(8,128)(2,1)S(1)}, u32[]{:S(2)}, u32[]{:S(2)}) collective-permute-start(bf16[256,128]{1,0:T(8,128)(2,1)S(1)} %get-tuple-element.34.down), channel_id=1, source_target_pairs={{32,64},{64,32},{96,128},{128,96},{160,192},{192,160},{224,256},{2... | collective-permute-start | bytes 196616 | tf_op jit(solution)/shard_map/ppermute | solution.py:368
  30.1 2.0 %shard_map.87 = (bf16[3200,256]{1,0:T(8,128)(2,1)S(1)}, bf16[64,1920]{1,0:T(8,128)(2,1)S(1)}, f32[512,256]{1,0:T(8,128)S(1)}, bf16[512,640]{1,0:T(8,128)(2,1)S(1)}, f32[512,256]{1,0:T(8,128)S(1)}) custom-call(bf16[1280,128]{1,0:T(8,128)(2,1)S(1)} %get-tuple-element.29.first, bf16[1280,128]{1,0:T(8,128)(2,1)S(1)} %get-tuple-element.35.before, ...), custom_call_target="tpu_custom_call" | custom-call | tf_op jit(solution)/shard_map/pallas_call | solution.py:406
  32.1 0.0 collective-permute-done.5.inner
  32.1 0.0 collective-permute-done.4.chips0
  32.1 0.0 collective-permute-done.3.chips1
  32.1 0.0 collective-permute-done.2.outer
  32.1 6.8 %shard_map.88 = (bf16[64,512]{1,0:T(8,128)(2,1)S(1)}, bf16[1024,128]{1,0:T(8,128)(2,1)S(1)}, bf16[1024,128]{1,0:T(8,128)(2,1)S(1)}) custom-call(bf16[256,128]{1,0:T(8,128)(2,1)S(1)} %collective-permute-done.2.outer, bf16[256,128]{1,0:T(8,128)(2,1)S(1)} %collective-permute-done.3.chips1, bf16[256,128]{1,0:T(8,128)(2,1)S(1)} %collective-permute-done.4.chips0, ...), custom_call_target="tpu_custom_call" | custom-call | tf_op jit(solution)/shard_map/pallas_call | solution.py:418
  38.9 1.9 %collective-permute-start.6 = (bf16[1024,128]{1,0:T(8,128)(2,1)S(1)}, bf16[1024,128]{1,0:T(8,128)(2,1)S(1)}, u32[]{:S(2)}, u32[]{:S(2)}) collective-permute-start(bf16[1024,128]{1,0:T(8,128)(2,1)S(1)} %get-tuple-element.46), channel_id=1, source_target_pairs={{0,32},{32,0},{64,96},{96,64},{128,160},{160,128},{192,224},{224,1... | collective-permute-start | bytes 786440 | tf_op jit(solution)/shard_map/ppermute | solution.py:368
  40.9 1.5 %collective-permute-done.6 = bf16[1024,128]{1,0:T(8,128)(2,1)S(1)} collective-permute-done((bf16[1024,128]{1,0:T(8,128)(2,1)S(1)}, bf16[1024,128]{1,0:T(8,128)(2,1)S(1)}, u32[]{:S(2)}, u32[]{:S(2)}) %collective-permute-start.6) | collective-permute-done | bytes 262176 | tf_op jit(solution)/shard_map/ppermute | solution.py:368
  42.4 0.1 add_convert_fusion
  42.4 21.3 %all_to_all.15 = bf16[32,32,128]{2,1,0:T(8,128)(2,1)S(1)} all-to-all(bf16[32,32,128]{2,1,0:T(8,128)(2,1)S(1)} %bitcast.10), channel_id=1, replica_groups=mesh['space'=16,'dp'=32] {'dp'}, dimensions={0} | all-to-all | bytes 524288 | tf_op jit(solution)/shard_map/all_to_all | solution.py:355
  63.7 0.1 reduce_sum.24
  63.8 12.5 %all_to_all.16 = bf16[8,32,128]{2,1,0:T(8,128)(2,1)S(1)} all-to-all(bf16[8,32,128]{2,1,0:T(8,128)(2,1)S(1)} %broadcast_in_dim.4), channel_id=1, replica_groups={{0,64,128,192,256,320,384,448},{32,96,160,224,288,352,416,480},{1,65,12..., dimensions={0} | all-to-all | bytes 131072 | tf_op jit(solution)/shard_map/all_to_all | solution.py:361
  76.4 14.7 %all_to_all.17 = bf16[32,32,128]{2,1,0:T(8,128)(2,1)S(1)} all-to-all(bf16[32,32,128]{2,1,0:T(8,128)(2,1)S(1)} %broadcast_in_dim.5), channel_id=1, replica_groups=mesh['space'=16,'dp'=32] {'dp'}, dimensions={0} | all-to-all | bytes 524288 | tf_op jit(solution)/shard_map/all_to_all | solution.py:361
  91.1 6.0 %collective-permute-start.7 = (bf16[1024,128]{1,0:T(8,128)(2,1)S(1)}, bf16[1024,128]{1,0:T(8,128)(2,1)S(1)}, u32[]{:S(2)}, u32[]{:S(2)}) collective-permute-start(bf16[1024,128]{1,0:T(8,128)(2,1)S(1)} %bitcast.8), channel_id=1, source_target_pairs={{0,32},{32,0},{64,96},{96,64},{128,160},{160,128},{192,224},{224,1... | collective-permute-start | bytes 786440 | tf_op jit(solution)/shard_map/ppermute | solution.py:368
  97.1 0.8 reshape.39
  97.8 0.4 collective-permute-done.7.other
  98.2 1.5 %shard_map.89 = (f32[3,3,3,64,64]{4,3,2,1,0:T(8,128)}, f32[2,2,2,64,64]{4,3,2,1,0:T(8,128)}, f32[3,3,3,64,64]{4,3,2,1,0:T(8,128)}) custom-call(bf16[1024,128]{1,0:T(8,128)(2,1)S(1)} %bitcast.9, bf16[1024,128]{1,0:T(8,128)(2,1)S(1)} %collective-permute-done.7.other), custom_call_target="tpu_custom_call" | custom-call | tf_op jit(solution)/shard_map/pallas_call | solution.py:435
  (3 shorter events, 0.1 us)
Async XLA Ops:
  2.3 12.5 %collective-permute-start = (bf16[1280,128]{1,0:T(8,128)(2,1)S(1)}, bf16[1280,128]{1,0:T(8,128)(2,1)S(1)}, u32[]{:S(2)}, u32[]{:S(2)}) collective-permute-start(bf16[1280,128]{1,0:T(8,128)(2,1)S(1)} %get-tuple-element.27), channel_id=1, source_target_pairs={{32,64},{64,32},{96,128},{128,96},{160,192},{192,160},{224,256},{2... | collective-permute-start | bytes 983048 | tf_op jit(solution)/shard_map/ppermute | solution.py:368
  7.7 7.1 %collective-permute-start.1 = (bf16[1280,128]{1,0:T(8,128)(2,1)S(1)}, bf16[1280,128]{1,0:T(8,128)(2,1)S(1)}, u32[]{:S(2)}, u32[]{:S(2)}) collective-permute-start(bf16[1280,128]{1,0:T(8,128)(2,1)S(1)} %get-tuple-element.28), channel_id=1, source_target_pairs={{0,32},{32,0},{64,96},{96,64},{128,160},{160,128},{192,224},{224,1... | collective-permute-start | bytes 983048 | tf_op jit(solution)/shard_map/ppermute | solution.py:368
  16.2 15.9 %collective-permute-start.5 = (bf16[256,128]{1,0:T(8,128)(2,1)S(1)}, bf16[256,128]{1,0:T(8,128)(2,1)S(1)}, u32[]{:S(2)}, u32[]{:S(2)}) collective-permute-start(bf16[256,128]{1,0:T(8,128)(2,1)S(1)} %get-tuple-element.34.down), channel_id=1, source_target_pairs={{0,32},{32,0},{64,96},{96,64},{128,160},{160,128},{192,224},{224,1... | collective-permute-start | bytes 196616 | tf_op jit(solution)/shard_map/ppermute | solution.py:368
  18.1 14.0 %collective-permute-start.4 = (bf16[256,128]{1,0:T(8,128)(2,1)S(1)}, bf16[256,128]{1,0:T(8,128)(2,1)S(1)}, u32[]{:S(2)}, u32[]{:S(2)}) collective-permute-start(bf16[256,128]{1,0:T(8,128)(2,1)S(1)} %get-tuple-element.34.down), channel_id=1, source_target_pairs={{0,64},{64,0},{32,96},{96,32},{128,192},{192,128},{160,224},{224,1... | collective-permute-start | bytes 196616 | tf_op jit(solution)/shard_map/ppermute | solution.py:368
  20.4 11.7 %collective-permute-start.3 = (bf16[256,128]{1,0:T(8,128)(2,1)S(1)}, bf16[256,128]{1,0:T(8,128)(2,1)S(1)}, u32[]{:S(2)}, u32[]{:S(2)}) collective-permute-start(bf16[256,128]{1,0:T(8,128)(2,1)S(1)} %get-tuple-element.34.down), channel_id=1, source_target_pairs={{64,128},{128,64},{96,160},{160,96},{192,256},{256,192},{224,288},... | collective-permute-start | bytes 196616 | tf_op jit(solution)/shard_map/ppermute | solution.py:368
  21.1 11.0 %collective-permute-start.2 = (bf16[256,128]{1,0:T(8,128)(2,1)S(1)}, bf16[256,128]{1,0:T(8,128)(2,1)S(1)}, u32[]{:S(2)}, u32[]{:S(2)}) collective-permute-start(bf16[256,128]{1,0:T(8,128)(2,1)S(1)} %get-tuple-element.34.down), channel_id=1, source_target_pairs={{32,64},{64,32},{96,128},{128,96},{160,192},{192,160},{224,256},{2... | collective-permute-start | bytes 196616 | tf_op jit(solution)/shard_map/ppermute | solution.py:368
  38.9 3.4 %collective-permute-start.6 = (bf16[1024,128]{1,0:T(8,128)(2,1)S(1)}, bf16[1024,128]{1,0:T(8,128)(2,1)S(1)}, u32[]{:S(2)}, u32[]{:S(2)}) collective-permute-start(bf16[1024,128]{1,0:T(8,128)(2,1)S(1)} %get-tuple-element.46), channel_id=1, source_target_pairs={{0,32},{32,0},{64,96},{96,64},{128,160},{160,128},{192,224},{224,1... | collective-permute-start | bytes 786440 | tf_op jit(solution)/shard_map/ppermute | solution.py:368
  91.1 7.1 %collective-permute-start.7 = (bf16[1024,128]{1,0:T(8,128)(2,1)S(1)}, bf16[1024,128]{1,0:T(8,128)(2,1)S(1)}, u32[]{:S(2)}, u32[]{:S(2)}) collective-permute-start(bf16[1024,128]{1,0:T(8,128)(2,1)S(1)} %bitcast.8), channel_id=1, source_target_pairs={{0,32},{32,0},{64,96},{96,64},{128,160},{160,128},{192,224},{224,1... | collective-permute-start | bytes 786440 | tf_op jit(solution)/shard_map/ppermute | solution.py:368

commit v6 on v4

--- a/solution.py
+++ b/solution.py
@@ -148,7 +148,7 @@
         part[x * 512 : x * 512 + 512] = dot(taps[...], fw[1024 - x * 1024 : 3072 - x * 1024])
 
 
-def first_kernel(outer, inner, part, fw, dw, act, pre, send, before, after, taps):
+def first_kernel(outer, inner, part, fw, dw, act, slope, send, before, after, taps):
     low = low_lanes((256, 128))
     even = core() == 0
     before[...] = jnp.where(even, outer[...], inner[...])
@@ -156,20 +156,18 @@
     for x, side in enumerate((before, after)):
         gather_taps(side[0:1024], taps)
         value = part[x * 512 : x * 512 + 512] + dot(taps[...], fw[x * 2048 : x * 2048 + 1024])
-        pre[x * 512 : x * 512 + 512] = value
-        act[:, x * 256 : x * 256 + 256] = (value * jax.nn.sigmoid(value)).astype(BF16)
+        s = jax.nn.sigmoid(value)
+        slope[x * 512 : x * 512 + 512] = s * (1.0 + value * (1.0 - s))
+        act[:, x * 256 : x * 256 + 256] = (value * s).astype(BF16)
     down = dot(act[...], dw[...])
     send[...] = jnp.where(low, down[:256], down[256:]).astype(BF16)
 
 
 def beside_kernel(
-    first, before, after, pre, down, far_coarse, cw, bw, slope, ct, own, acc, w_coarse, sem
+    first, before, after, down, far_coarse, cw, bw, ct, own, acc, w_coarse, sem
 ):
     copy = pltpu.make_async_copy(far_coarse, w_coarse, sem)
     copy.start()
-    value = pre[...]
-    s = jax.nn.sigmoid(value)
-    slope[...] = s * (1.0 + value * (1.0 - s))
     low = low_lanes((256, 128))
     f0, t0 = turned(before[1024:1280])
     f1, t1 = turned(first[1024:1280])
@@ -210,7 +208,7 @@
 
 
 def rest_kernel(
-    outer, chips1, chips0, inner, first, last, before, after, act, slope, ct, own, acc, dw, cw, bw, out, keep, send,
+    inner, chips0, chips1, outer, first, last, before, after, act, slope, ct, own, acc, dw, cw, bw, out, keep, send,
     grads, below, above, near, taps,
 ):
     low = low_lanes((64, 128))
@@ -388,26 +386,25 @@
         [((512, 2048), BF16), ((1728, 64), BF16), ((512, 64), BF16), pltpu.SemaphoreType.DMA((2,))],
         "vvhh",
     )(first, last, far(w_first.reshape(1728, 64)), far(w_down.reshape(512, 64)))
-    act, pre, down, before, after = call(
+    act, slope, down, before, after = call(
         first_kernel,
         [((512, 512), BF16), ((1024, 256), F32), ((256, 128), BF16)] + [((1280, 128), BF16)] * 2,
         [((512, 1024), BF16)],
         "vvvvv",
     )(outer, inner, part, fw, dw)
-    halo = [swap(down, pairs) for pairs in (across, beside[1], beside[0], chip)]
-    cw, bw, slope, ct, own, acc = call(
+    halo = [swap(down, pairs) for pairs in (chip, beside[0], beside[1], across)]
+    cw, bw, ct, own, acc = call(
         beside_kernel,
         [
             ((3200, 256), BF16),
             ((64, 1920), BF16),
-            ((1024, 256), F32),
             ((512, 256), F32),
             ((512, 640), BF16),
             ((512, 256), F32),
         ],
         [((1728, 64), BF16), pltpu.SemaphoreType.DMA],
-        "vvvvvh",
-    )(first, before, after, pre, down, far(w_coarse.reshape(1728, 64)))
+        "vvvvh",
+    )(first, before, after, down, far(w_coarse.reshape(1728, 64)))
     out, keep, send = call(
         rest_kernel,
         [((64, 512), BF16), ((1024, 128), BF16), ((1024, 128), BF16)],

time: 99.8 us -> 99.8 us (level)
  no operation moved by 1% of the time
where the time goes in v6:
time: 99.8 us; the launch traced here: 99.4 us
  blocking collectives  48.9 us (49%)
  starting transfers between devices  31.2 us (31%)
  Pallas kernels  16 us (16%)
  waiting for transfers between devices  1.51 us (2%)
    ppermute x8, starting transfers between devices, swap(): lax.ppermute(value, 'space', [p for i, j in pairs for p in ((i, j), (j, i...  31.2 us
    all_to_all x2, blocking collectives, spread(): return lax.all_to_all(y, axis, 0, 0, tiled=True, axis_index_groups=groups)  27.9 us
    all_to_all x1, blocking collectives, scatter_sum(): y = lax.all_to_all(y, axis, 0, 0, tiled=True, axis_index_groups=groups)  21.1 us
    pallas_call x1, Pallas kernels, local(): call(rest_kernel, [((64, 512), BF16), ((1024, 128), BF16), ((1024, 128),...  6.8 us
    pallas_call x1, Pallas kernels, local(): call(prepare_kernel, [((1024, 256), F32), ((3072, 256), BF16), ((512, 128...  2.81 us
  transfers between devices with their start and end apart: 8, of which 2 were waited for; matrix products, arithmetic and copies ran while one was open for 1% of the time, Pallas kernels for 5%

profile of v6, /device:TPU:1, one launch (start us, length us, event | category | flops | bytes accessed | tf_op | source)
XLA Modules:
  0.0 99.4 jit_solution(4644452830912482293)
XLA Ops:
  0.6 1.6 %shard_map.84 = (bf16[1280,128]{1,0:T(8,128)(2,1)S(1)}, bf16[1280,128]{1,0:T(8,128)(2,1)S(1)}, bf16[1280,128]{1,0:T(8,128)(2,1)S(1)}, bf16[1280,128]{1,0:T(8,128)(2,1)S(1)}) custom-call(bf16[64,2,16,128]{3,2,1,0:T(8,128)(2,1)} %bitcast.11, bf16[64,8,64]{2,1,0:T(8,128)(2,1)} %bitcast.14), custom_call_target="tpu_custom_call" | custom-call | tf_op jit(solution)/shard_map/pallas_call | solution.py:370
  2.3 5.4 %collective-permute-start = (bf16[1280,128]{1,0:T(8,128)(2,1)S(1)}, bf16[1280,128]{1,0:T(8,128)(2,1)S(1)}, u32[]{:S(2)}, u32[]{:S(2)}) collective-permute-start(bf16[1280,128]{1,0:T(8,128)(2,1)S(1)} %get-tuple-element.27), channel_id=1, source_target_pairs={{32,64},{64,32},{96,128},{128,96},{160,192},{192,160},{224,256},{2... | collective-permute-start | bytes 983048 | tf_op jit(solution)/shard_map/ppermute | solution.py:365
  7.7 4.1 %collective-permute-start.1 = (bf16[1280,128]{1,0:T(8,128)(2,1)S(1)}, bf16[1280,128]{1,0:T(8,128)(2,1)S(1)}, u32[]{:S(2)}, u32[]{:S(2)}) collective-permute-start(bf16[1280,128]{1,0:T(8,128)(2,1)S(1)} %get-tuple-element.28), channel_id=1, source_target_pairs={{0,32},{32,0},{64,96},{96,64},{128,160},{160,128},{192,224},{224,1... | collective-permute-start | bytes 983048 | tf_op jit(solution)/shard_map/ppermute | solution.py:365
  11.8 2.8 %shard_map.85 = (f32[1024,256]{1,0:T(8,128)S(1)}, bf16[3072,256]{1,0:T(8,128)(2,1)S(1)}, bf16[512,128]{1,0:T(8,128)(2,1)S(1)}) custom-call(bf16[1280,128]{1,0:T(8,128)(2,1)S(1)} %get-tuple-element.29.first, bf16[1280,128]{1,0:T(8,128)(2,1)S(1)} %get-tuple-element.30.last, bf16[1728,64]{1,0:T(8,128)(2,1)} %bitcast.12, bf16[512,64]{1,0:T(8,128)(2,1)} %bitcast.15), custom_call_target="tpu_custom_call" | custom-call | tf_op jit(solution)/shard_map/pallas_call | solution.py:383
  14.6 0.0 collective-permute-done.outer
  14.6 0.0 collective-permute-done.1.inner
  14.6 1.4 %shard_map.86 = (bf16[512,512]{1,0:T(8,128)(2,1)S(1)}, f32[1024,256]{1,0:T(8,128)S(1)}, bf16[256,128]{1,0:T(8,128)(2,1)S(1)}, bf16[1280,128]{1,0:T(8,128)(2,1)S(1)}, bf16[1280,128]{1,0:T(8,128)(2,1)S(1)}) custom-call(bf16[1280,128]{1,0:T(8,128)(2,1)S(1)} %collective-permute-done.outer, bf16[1280,128]{1,0:T(8,128)(2,1)S(1)} %collective-permute-done.1.inner, ...), custom_call_target="tpu_custom_call" | custom-call | tf_op jit(solution)/shard_map/pallas_call | solution.py:389
  16.0 2.2 %collective-permute-start.5 = (bf16[256,128]{1,0:T(8,128)(2,1)S(1)}, bf16[256,128]{1,0:T(8,128)(2,1)S(1)}, u32[]{:S(2)}, u32[]{:S(2)}) collective-permute-start(bf16[256,128]{1,0:T(8,128)(2,1)S(1)} %get-tuple-element.34.down), channel_id=1, source_target_pairs={{32,64},{64,32},{96,128},{128,96},{160,192},{192,160},{224,256},{2... | collective-permute-start | bytes 196616 | tf_op jit(solution)/shard_map/ppermute | solution.py:365
  18.2 0.7 collective-permute-start.4
  18.9 8.6 %collective-permute-start.3 = (bf16[256,128]{1,0:T(8,128)(2,1)S(1)}, bf16[256,128]{1,0:T(8,128)(2,1)S(1)}, u32[]{:S(2)}, u32[]{:S(2)}) collective-permute-start(bf16[256,128]{1,0:T(8,128)(2,1)S(1)} %get-tuple-element.34.down), channel_id=1, source_target_pairs={{0,64},{64,0},{32,96},{96,32},{128,192},{192,128},{160,224},{224,1... | collective-permute-start | bytes 196616 | tf_op jit(solution)/shard_map/ppermute | solution.py:365
  27.5 1.9 %collective-permute-start.2 = (bf16[256,128]{1,0:T(8,128)(2,1)S(1)}, bf16[256,128]{1,0:T(8,128)(2,1)S(1)}, u32[]{:S(2)}, u32[]{:S(2)}) collective-permute-start(bf16[256,128]{1,0:T(8,128)(2,1)S(1)} %get-tuple-element.34.down), channel_id=1, source_target_pairs={{0,32},{32,0},{64,96},{96,64},{128,160},{160,128},{192,224},{224,1... | collective-permute-start | bytes 196616 | tf_op jit(solution)/shard_map/ppermute | solution.py:365
  29.4 1.8 %shard_map.87 = (bf16[3200,256]{1,0:T(8,128)(2,1)S(1)}, bf16[64,1920]{1,0:T(8,128)(2,1)S(1)}, f32[512,256]{1,0:T(8,128)S(1)}, bf16[512,640]{1,0:T(8,128)(2,1)S(1)}, f32[512,256]{1,0:T(8,128)S(1)}) custom-call(bf16[1280,128]{1,0:T(8,128)(2,1)S(1)} %get-tuple-element.29.first, bf16[1280,128]{1,0:T(8,128)(2,1)S(1)} %get-tuple-element.35.before, ...), custom_call_target="tpu_custom_call" | custom-call | tf_op jit(solution)/shard_map/pallas_call | solution.py:396
  31.2 0.0 collective-permute-done.5.outer
  31.2 0.0 collective-permute-done.4.chips1
  31.2 0.0 collective-permute-done.3.chips0
  31.2 0.0 collective-permute-done.2.inner
  31.2 6.8 %shard_map.88 = (bf16[64,512]{1,0:T(8,128)(2,1)S(1)}, bf16[1024,128]{1,0:T(8,128)(2,1)S(1)}, bf16[1024,128]{1,0:T(8,128)(2,1)S(1)}) custom-call(bf16[256,128]{1,0:T(8,128)(2,1)S(1)} %collective-permute-done.2.inner, bf16[256,128]{1,0:T(8,128)(2,1)S(1)} %collective-permute-done.3.chips0, bf16[256,128]{1,0:T(8,128)(2,1)S(1)} %collective-permute-done.4.chips1, ...), custom_call_target="tpu_custom_call" | custom-call | tf_op jit(solution)/shard_map/pallas_call | solution.py:408
  38.0 2.4 %collective-permute-start.6 = (bf16[1024,128]{1,0:T(8,128)(2,1)S(1)}, bf16[1024,128]{1,0:T(8,128)(2,1)S(1)}, u32[]{:S(2)}, u32[]{:S(2)}) collective-permute-start(bf16[1024,128]{1,0:T(8,128)(2,1)S(1)} %get-tuple-element.46), channel_id=1, source_target_pairs={{0,32},{32,0},{64,96},{96,64},{128,160},{160,128},{192,224},{224,1... | collective-permute-start | bytes 786440 | tf_op jit(solution)/shard_map/ppermute | solution.py:365
  40.4 1.1 %collective-permute-done.6 = bf16[1024,128]{1,0:T(8,128)(2,1)S(1)} collective-permute-done((bf16[1024,128]{1,0:T(8,128)(2,1)S(1)}, bf16[1024,128]{1,0:T(8,128)(2,1)S(1)}, u32[]{:S(2)}, u32[]{:S(2)}) %collective-permute-start.6) | collective-permute-done | bytes 262176 | tf_op jit(solution)/shard_map/ppermute | solution.py:365
  41.6 0.1 add_convert_fusion
  41.6 21.1 %all_to_all.15 = bf16[32,32,128]{2,1,0:T(8,128)(2,1)S(1)} all-to-all(bf16[32,32,128]{2,1,0:T(8,128)(2,1)S(1)} %bitcast.10), channel_id=1, replica_groups=mesh['space'=16,'dp'=32] {'dp'}, dimensions={0} | all-to-all | bytes 524288 | tf_op jit(solution)/shard_map/all_to_all | solution.py:352
  62.7 0.1 reduce_sum.24
  62.8 12.9 %all_to_all.16 = bf16[8,32,128]{2,1,0:T(8,128)(2,1)S(1)} all-to-all(bf16[8,32,128]{2,1,0:T(8,128)(2,1)S(1)} %broadcast_in_dim.4), channel_id=1, replica_groups={{0,64,128,192,256,320,384,448},{32,96,160,224,288,352,416,480},{1,65,12..., dimensions={0} | all-to-all | bytes 131072 | tf_op jit(solution)/shard_map/all_to_all | solution.py:358
  75.8 15.0 %all_to_all.17 = bf16[32,32,128]{2,1,0:T(8,128)(2,1)S(1)} all-to-all(bf16[32,32,128]{2,1,0:T(8,128)(2,1)S(1)} %broadcast_in_dim.5), channel_id=1, replica_groups=mesh['space'=16,'dp'=32] {'dp'}, dimensions={0} | all-to-all | bytes 524288 | tf_op jit(solution)/shard_map/all_to_all | solution.py:358
  90.7 6.0 %collective-permute-start.7 = (bf16[1024,128]{1,0:T(8,128)(2,1)S(1)}, bf16[1024,128]{1,0:T(8,128)(2,1)S(1)}, u32[]{:S(2)}, u32[]{:S(2)}) collective-permute-start(bf16[1024,128]{1,0:T(8,128)(2,1)S(1)} %bitcast.8), channel_id=1, source_target_pairs={{0,32},{32,0},{64,96},{96,64},{128,160},{160,128},{192,224},{224,1... | collective-permute-start | bytes 786440 | tf_op jit(solution)/shard_map/ppermute | solution.py:365
  96.7 0.8 reshape.39
  97.5 0.4 collective-permute-done.7.other
  97.8 1.5 %shard_map.89 = (f32[3,3,3,64,64]{4,3,2,1,0:T(8,128)}, f32[2,2,2,64,64]{4,3,2,1,0:T(8,128)}, f32[3,3,3,64,64]{4,3,2,1,0:T(8,128)}) custom-call(bf16[1024,128]{1,0:T(8,128)(2,1)S(1)} %bitcast.9, bf16[1024,128]{1,0:T(8,128)(2,1)S(1)} %collective-permute-done.7.other), custom_call_target="tpu_custom_call" | custom-call | tf_op jit(solution)/shard_map/pallas_call | solution.py:425
  (3 shorter events, 0.1 us)
Async XLA Ops:
  2.3 12.3 %collective-permute-start = (bf16[1280,128]{1,0:T(8,128)(2,1)S(1)}, bf16[1280,128]{1,0:T(8,128)(2,1)S(1)}, u32[]{:S(2)}, u32[]{:S(2)}) collective-permute-start(bf16[1280,128]{1,0:T(8,128)(2,1)S(1)} %get-tuple-element.27), channel_id=1, source_target_pairs={{32,64},{64,32},{96,128},{128,96},{160,192},{192,160},{224,256},{2... | collective-permute-start | bytes 983048 | tf_op jit(solution)/shard_map/ppermute | solution.py:365
  7.7 6.9 %collective-permute-start.1 = (bf16[1280,128]{1,0:T(8,128)(2,1)S(1)}, bf16[1280,128]{1,0:T(8,128)(2,1)S(1)}, u32[]{:S(2)}, u32[]{:S(2)}) collective-permute-start(bf16[1280,128]{1,0:T(8,128)(2,1)S(1)} %get-tuple-element.28), channel_id=1, source_target_pairs={{0,32},{32,0},{64,96},{96,64},{128,160},{160,128},{192,224},{224,1... | collective-permute-start | bytes 983048 | tf_op jit(solution)/shard_map/ppermute | solution.py:365
  16.0 15.2 %collective-permute-start.5 = (bf16[256,128]{1,0:T(8,128)(2,1)S(1)}, bf16[256,128]{1,0:T(8,128)(2,1)S(1)}, u32[]{:S(2)}, u32[]{:S(2)}) collective-permute-start(bf16[256,128]{1,0:T(8,128)(2,1)S(1)} %get-tuple-element.34.down), channel_id=1, source_target_pairs={{32,64},{64,32},{96,128},{128,96},{160,192},{192,160},{224,256},{2... | collective-permute-start | bytes 196616 | tf_op jit(solution)/shard_map/ppermute | solution.py:365
  18.2 12.9 %collective-permute-start.4 = (bf16[256,128]{1,0:T(8,128)(2,1)S(1)}, bf16[256,128]{1,0:T(8,128)(2,1)S(1)}, u32[]{:S(2)}, u32[]{:S(2)}) collective-permute-start(bf16[256,128]{1,0:T(8,128)(2,1)S(1)} %get-tuple-element.34.down), channel_id=1, source_target_pairs={{64,128},{128,64},{96,160},{160,96},{192,256},{256,192},{224,288},... | collective-permute-start | bytes 196616 | tf_op jit(solution)/shard_map/ppermute | solution.py:365
  18.9 12.3 %collective-permute-start.3 = (bf16[256,128]{1,0:T(8,128)(2,1)S(1)}, bf16[256,128]{1,0:T(8,128)(2,1)S(1)}, u32[]{:S(2)}, u32[]{:S(2)}) collective-permute-start(bf16[256,128]{1,0:T(8,128)(2,1)S(1)} %get-tuple-element.34.down), channel_id=1, source_target_pairs={{0,64},{64,0},{32,96},{96,32},{128,192},{192,128},{160,224},{224,1... | collective-permute-start | bytes 196616 | tf_op jit(solution)/shard_map/ppermute | solution.py:365
  27.5 3.7 %collective-permute-start.2 = (bf16[256,128]{1,0:T(8,128)(2,1)S(1)}, bf16[256,128]{1,0:T(8,128)(2,1)S(1)}, u32[]{:S(2)}, u32[]{:S(2)}) collective-permute-start(bf16[256,128]{1,0:T(8,128)(2,1)S(1)} %get-tuple-element.34.down), channel_id=1, source_target_pairs={{0,32},{32,0},{64,96},{96,64},{128,160},{160,128},{192,224},{224,1... | collective-permute-start | bytes 196616 | tf_op jit(solution)/shard_map/ppermute | solution.py:365
  38.0 3.6 %collective-permute-start.6 = (bf16[1024,128]{1,0:T(8,128)(2,1)S(1)}, bf16[1024,128]{1,0:T(8,128)(2,1)S(1)}, u32[]{:S(2)}, u32[]{:S(2)}) collective-permute-start(bf16[1024,128]{1,0:T(8,128)(2,1)S(1)} %get-tuple-element.46), channel_id=1, source_target_pairs={{0,32},{32,0},{64,96},{96,64},{128,160},{160,128},{192,224},{224,1... | collective-permute-start | bytes 786440 | tf_op jit(solution)/shard_map/ppermute | solution.py:365
  90.7 7.1 %collective-permute-start.7 = (bf16[1024,128]{1,0:T(8,128)(2,1)S(1)}, bf16[1024,128]{1,0:T(8,128)(2,1)S(1)}, u32[]{:S(2)}, u32[]{:S(2)}) collective-permute-start(bf16[1024,128]{1,0:T(8,128)(2,1)S(1)} %bitcast.8), channel_id=1, source_target_pairs={{0,32},{32,0},{64,96},{96,64},{128,160},{160,128},{192,224},{224,1... | collective-permute-start | bytes 786440 | tf_op jit(solution)/shard_map/ppermute | solution.py:365
